TPU v7x, 512 devices: a whole 4x4x16 slice. The times are simulated.
512 devices in a mesh: row: 64 (over z, y), col: 8 (over x, core).
Axes of the slice: x: 4, y: 4, z: 16, core: 2. Of those that a mesh axis runs over, the one named last changes fastest.
Arguments:
- panel: float32 [131072, 256], P('row', 'col'), may hold values from -0.022097087 to 0.022097087, as said below
- trailing: float32 [131072, 2048], P('row', 'col'), may hold values from -6 to 6
Outputs:
- factor: float32 [256, 256], P(None, 'col')
- coupling: float32 [256, 2048], P(None, 'col')
- updated: float32 [131072, 2048], P('row', 'col')
Inputs may be any that keep to these rules, and one draw needn't show every extreme that they name: A full-rank panel whose columns have norms of order one.
All inputs are finite; a program needn't handle non-finite values.
Results may differ from a plain program's by a relative error of at most 0.0003.
Values sent between devices are 32-bit elements; how exact they have to be, the bound alone decides.
A program may use at most 128 MiB of HBM per device.

v0:
```python
import jax
import jax.numpy as jnp
from jax import lax
from jax.sharding import PartitionSpec as P


def gram_of(left, right):
    return jnp.dot(
        left.T, right, precision=lax.Precision.HIGHEST, preferred_element_type=jnp.float32
    )


def upper_factor(gram):
    order = gram.shape[0]
    positions = jnp.arange(order)

    def column_step(index, carry):
        work, lower = carry
        pick = (positions == index).astype(jnp.float32)
        column = jnp.sum(work * pick[None, :], axis=1)
        pivot = jnp.sqrt(jnp.sum(column * pick))
        column = jnp.where(positions >= index, column / pivot, 0.0)
        lower = lower + column[:, None] * pick[None, :]
        work = work - column[:, None] * column[None, :]
        return (work, lower)

    start = (gram, jnp.zeros_like(gram))
    work, lower = lax.fori_loop(0, order, column_step, start)
    return lower.T


def upper_inverse(upper):
    order = upper.shape[0]
    positions = jnp.arange(order)

    def back_step(count, inverse):
        index = order - 1 - count
        pick = (positions == index).astype(jnp.float32)
        row_vals = jnp.sum(upper * pick[:, None], axis=0)
        pivot = jnp.sum(row_vals * pick)
        known = jnp.dot(
            row_vals, inverse, precision=lax.Precision.HIGHEST, preferred_element_type=jnp.float32
        )
        fresh = (pick - known) / pivot
        return inverse + pick[:, None] * fresh[None, :]

    return lax.fori_loop(0, order, back_step, jnp.zeros_like(upper))


def on_device(panel, trailing):
    whole = lax.all_gather(panel, "col", axis=1, tiled=True)
    gram_local = gram_of(whole, whole)
    cross_local = gram_of(whole, trailing)
    gram = lax.psum(gram_local, "row")
    factor = upper_factor(gram)
    cross = lax.psum(cross_local, "row")
    inverse = upper_inverse(factor)
    coupling = jnp.dot(
        inverse.T, cross, precision=lax.Precision.HIGHEST, preferred_element_type=jnp.float32
    )
    solved = jnp.dot(
        inverse, coupling, precision=lax.Precision.HIGHEST, preferred_element_type=jnp.float32
    )
    updated = trailing - jnp.dot(
        whole, solved, precision=lax.Precision.HIGHEST, preferred_element_type=jnp.float32
    )
    width = panel.shape[1]
    factor_cols = lax.dynamic_slice_in_dim(factor, lax.axis_index("col") * width, width, 1)
    return (factor_cols, coupling, updated)


def solution(mesh):
    in_specs = (P("row", "col"), P("row", "col"))
    out_specs = (P(None, "col"), P(None, "col"), P("row", "col"))
    return jax.shard_map(
        on_device, mesh=mesh, in_specs=in_specs, out_specs=out_specs, check_vma=False
    )
```

profile of v0, /device:TPU:1, one launch (start us, length us, event | category | flops | bytes accessed | tf_op | source)
XLA Modules:
  0.0 1842.3 jit_solution(3765235812296434401)
XLA Ops:
  7.9 40.8 %all-gather.2.cloned.1.call-done = f32[2048,256]{0,1:T(8,128)} async-done(((f32[2048,32]{0,1:T(8,128)}), f32[2048,256]{0,1:T(8,128)}) %all-gather.2.cloned.1.call-update) | async-done | bytes 2097168 | tf_op jit(solution)/shard_map/all_gather | solution.py:51
  48.7 4.9 fusion.16
  53.7 4.2 fusion.17
  57.9 2.9 copy.6
  60.8 253.3 %all-reduce.3.cloned.1.call-done = (f32[256,256]{1,0:T(8,128)}, f32[256,256]{1,0:T(8,128)}) async-done(((f32[256,256]{1,0:T(8,128)}, f32[256,256]{1,0:T(8,128)}), (f32[256,256]{1,0:T(8,128)}, f32[256,256]{1,0:T(8,128)})) %all-reduce.3.cloned.1.call-update) | async-done | bytes 524304 | tf_op jit(solution)/shard_map/psum | solution.py:54
  314.0 1061.1 %while.32 = (s32[]{:T(128)}, f32[256,256]{1,0:T(8,128)}, f32[256,256]{1,0:T(8,128)S(1)}, s32[]{:T(128)}, s32[]{:T(128)}) while((s32[]{:T(128)}, f32[256,256]{1,0:T(8,128)}, f32[256,256]{1,0:T(8,128)S(1)}, s32[]{:T(128)}, s32[]{:T(128)}) %tuple.71), condition=%wide.region_4.5_spmd.clone.clone, body=%wide.region_1.4_spmd.clone.clone.sunk | while | flops 460546 | bytes 1319019 | solution.py:28
  320.5 1.8 select_add_fusion.2
  324.7 1.8 select_add_fusion.2
  328.8 1.8 select_add_fusion.2
  345.4 1.8 select_add_fusion.2
  349.6 1.8 select_add_fusion.2
  353.7 1.8 select_add_fusion.2
  370.3 1.8 select_add_fusion.2
  374.4 1.8 select_add_fusion.2
  378.6 1.8 select_add_fusion.2
  382.7 1.8 select_add_fusion.2
  399.3 1.8 select_add_fusion.2
  403.4 1.8 select_add_fusion.2
  407.6 1.8 select_add_fusion.2
  424.2 1.8 select_add_fusion.2
  428.3 1.8 select_add_fusion.2
  432.5 1.8 select_add_fusion.2
  449.0 1.8 select_add_fusion.2
  453.2 1.8 select_add_fusion.2
  457.3 1.8 select_add_fusion.2
  461.5 1.8 select_add_fusion.2
  478.0 1.8 select_add_fusion.2
  482.2 1.8 select_add_fusion.2
  486.3 1.8 select_add_fusion.2
  502.9 1.8 select_add_fusion.2
  507.1 1.8 select_add_fusion.2
  511.2 1.8 select_add_fusion.2
  527.8 1.8 select_add_fusion.2
  531.9 1.8 select_add_fusion.2
  536.1 1.8 select_add_fusion.2
  540.2 1.8 select_add_fusion.2
  556.8 1.8 select_add_fusion.2
  560.9 1.8 select_add_fusion.2
  565.1 1.8 select_add_fusion.2
  581.7 1.8 select_add_fusion.2
  585.8 1.8 select_add_fusion.2
  590.0 1.8 select_add_fusion.2
  606.5 1.8 select_add_fusion.2
  610.7 1.8 select_add_fusion.2
  614.8 1.8 select_add_fusion.2
  1375.8 450.8 %while.31 = (s32[]{:T(128)}, f32[256,256]{1,0:T(8,128)S(1)}, f32[256,256]{1,0:T(8,128)S(1)}, s32[]{:T(128)}, s32[]{:T(128)}, /*index=5*/s32[]{:T(128)}) while((s32[]{:T(128)}, f32[256,256]{1,0:T(8,128)S(1)}, f32[256,256]{1,0:T(8,128)S(1)}, s32[]{:T(128)}, s32[]{:T(128)}, /*index=5*/s32[]{:T(128)}) %tuple.74), condition=%wide.region_8.0_spmd.clone, body=%wide.region_5.8_spmd.clone.sunk | while | flops 1181699 | bytes 1058936 | solution.py:47
  1827.7 4.9 fusion.15
  1832.6 2.9 copy.7
  (2793 shorter events, 1254.0 us)
Async XLA Ops:
  7.2 41.5 %all-gather.2.cloned.1.call-start = ((), (), s32[]{:S(2)}) async-start(), calls=%async_computation | async-start | bytes 2359296 | tf_op jit(solution)/shard_map/all_gather | solution.py:51
  7.9 306.1 %all-reduce.3.cloned.1.call-start = ((), (), s32[]{:S(2)}) async-start(), calls=%async_computation.1 | async-start | bytes 1048576 | tf_op jit(solution)/shard_map/psum | solution.py:54
  48.7 4.9 copy-start
  1375.8 450.8 %copy-start.2 = (f32[256,256]{1,0:T(8,128)S(1)}, f32[256,256]{1,0:T(8,128)}, u32[]{:S(2)}) copy-start(f32[256,256]{1,0:T(8,128)} %get-tuple-element.225) | copy-start | bytes 786436
  1827.3 5.3 copy-start.1
Sparse Core Ops, SparseCore 0:
  10.1 38.5 all-gather.1
  58.0 256.0 all-reduce.2
where the time goes:
time: 1870 us; the launch traced here: 1840 us
  other arithmetic  1270 us (68%)
  waiting for transfers between devices  295 us (16%)
  loops' own time  192 us (10%)
  matrix products  63.5 us (3%)
    add x256, other arithmetic, column_step(): lower = lower + column[:, None] * pick[None, :]  452 us
    reduce_sum x256, other arithmetic, column_step(): column = jnp.sum(work * pick[None, :], axis=1)  272 us
    psum x1, waiting for transfers between devices, on_device(): gram = lax.psum(gram_local, 'row')  253 us
    another operation x1, loops' own time, upper_factor(): work, lower = lax.fori_loop(0, order, column_step, start)  181 us
    div x256, other arithmetic, back_step(): fresh = (pick - known) / pivot  177 us
    reduce_sum x256, other arithmetic, back_step(): pivot = jnp.sum(row_vals * pick)  155 us
    reduce_sum x256, other arithmetic, column_step(): pivot = jnp.sqrt(jnp.sum(column * pick))  155 us
    dot_general x256, matrix products, back_step(): jnp.dot(row_vals, inverse, precision=lax.Precision.HIGHEST, preferred_ele...  48.5 us
  transfers between devices with their start and end apart: 2, of which 2 were waited for; matrix products, arithmetic and copies ran while one was open for 0% of the time, Pallas kernels for 0%

commit v1 on v0

v1 whole, which is shorter than its diff:
```python
import functools

import jax
import jax.numpy as jnp
from jax import lax
from jax.experimental import pallas as pl
from jax.experimental.pallas import tpu as pltpu
from jax.sharding import PartitionSpec as P

F32 = jnp.float32
BF16 = jnp.bfloat16
HIGHEST = lax.Precision.HIGHEST
MESH = pl.DeviceIdType.MESH
STEP = 16
LANES = 128


def split(value):
    high = value.astype(BF16)
    low = (value - high.astype(F32)).astype(BF16)
    return high, low


def dot3(left, right, dims):
    left_hi, left_lo = split(left)
    right_hi, right_lo = split(right)
    dot = functools.partial(
        lax.dot_general, dimension_numbers=(dims, ((), ())), preferred_element_type=F32
    )
    return dot(left_hi, right_hi) + (dot(left_hi, right_lo) + dot(left_lo, right_hi))


def remote(src, dst, send, recv, where):
    return pltpu.make_async_remote_copy(
        src_ref=src, dst_ref=dst, send_sem=send, recv_sem=recv, device_id=where, device_id_type=MESH
    )


def reduce_kernel(
    pt, tr, whole_out, gram_out, cross_out,
    whole, trail, gram_part, gram_y, gram_za, gram_zb, gram_full,
    cross_part, cross_y, cross_s, cross_z, cross_full,
    loc_sem, px_s, px_r, sb_s, sb_r, gy_s, gy_r, ga_s, ga_r, gb_s, gb_r, gf_s, gf_r,
    cy_s, cy_r, cz_s, cz_r, cg_s, cg_r, cf_s, cf_r,
):
    row, col = lax.axis_index("row"), lax.axis_index("col")
    z, y = row // 4, row % 4
    x, core = col // 2, col % 2
    zh, zl = z // 4, z % 4

    def at_y(d):
        return (z * 4 + (y + d) % 4, col)

    def at_z(d):
        return (((z + d) % 16) * 4 + y, col)

    def at_plane(d):
        spot = (y * 8 + col + d) % 32
        return (z * 4 + spot // 8, spot % 8)

    barrier = pltpu.get_barrier_semaphore()

    @pl.loop(1, 32)
    def _(d):
        pl.semaphore_signal(barrier, inc=1, device_id=at_plane(d), device_id_type=MESH)

    @pl.loop(1, 16)
    def _(d):
        pl.semaphore_signal(barrier, inc=1, device_id=at_z(d), device_id_type=MESH)

    pl.semaphore_wait(barrier, 46)

    half = pt.shape[1] // 2
    right, left = (row, ((x + 1) % 4) * 2 + core), (row, ((x + 3) % 4) * 2 + core)
    twin = (row, x * 2 + 1 - core)

    def slot(far, other, part):
        who = ((x + far) % 4) * 2 + (1 - core if other else core)
        return whole.at[pl.ds(pl.multiple_of(who * 32, 32), 32), pl.ds(part * half, half)]

    def own(part):
        return pt.at[:, pl.ds(part * half, half)]

    sends = {
        0: remote(own(0), slot(0, False, 0), px_s.at[0], px_r.at[0], right),
        1: remote(own(1), slot(0, False, 1), px_s.at[1], px_r.at[1], left),
        2: remote(own(1), slot(0, False, 1), px_s.at[2], px_r.at[2], right),
        3: remote(own(0), slot(0, False, 0), px_s.at[3], px_r.at[3], left),
    }
    for i in range(4):
        sends[i].start()
    to_twin = {}

    def relay(i, far, part, src=None):
        to_twin[i] = remote(
            slot(far, False, part) if src is None else src,
            slot(far, False, part), sb_s.at[i], sb_r.at[i], twin,
        )
        to_twin[i].start()

    relay(6, 0, 0, own(0))
    relay(7, 0, 1, own(1))
    mine = pltpu.make_async_copy(pt, whole.at[pl.ds(pl.multiple_of(col * 32, 32), 32), :], loc_sem.at[0])
    mine.start()
    load = pltpu.make_async_copy(tr, trail, loc_sem.at[1])
    load.start()

    sends[0].wait_recv()
    sends[4] = remote(slot(3, False, 0), slot(3, False, 0), px_s.at[4], px_r.at[4], right)
    sends[4].start()
    relay(0, 3, 0)
    sends[1].wait_recv()
    sends[5] = remote(slot(1, False, 1), slot(1, False, 1), px_s.at[5], px_r.at[5], left)
    sends[5].start()
    relay(1, 1, 1)
    sends[2].wait_recv()
    relay(2, 3, 1)
    sends[3].wait_recv()
    relay(3, 1, 0)
    sends[4].wait_recv()
    relay(4, 2, 0)
    sends[5].wait_recv()
    relay(5, 2, 1)
    mine.wait()
    load.wait()
    for i in range(8):
        to_twin[i].wait_recv()

    keep = pltpu.make_async_copy(whole, whole_out, loc_sem.at[2])
    keep.start()

    gram_part[...] = lax.dot_general(
        whole[pl.ds(pl.multiple_of(col * 32, 32), 32), :], whole[...],
        (((1,), (1,)), ((), ())), precision=HIGHEST, preferred_element_type=F32,
    )

    def eight(who):
        return pl.ds(pl.multiple_of(who * 8, 8), 8)

    def gram_y_copy(d):
        return remote(gram_part.at[eight((y + d) % 4)], gram_y.at[d], gy_s.at[d], gy_r.at[d], at_y(d))

    for d in range(1, 4):
        gram_y_copy(d).start()

    chunk = 512
    cross_part[...] = jnp.zeros_like(cross_part)

    @pl.loop(0, pt.shape[1] // chunk)
    def _(i):
        rows = pl.ds(pl.multiple_of(i * chunk, chunk), chunk)
        cross_part[...] += dot3(whole[:, rows], trail[rows, :], ((1,), (0,)))

    def cross_y_copy(d):
        return remote(
            cross_part.at[pl.ds(pl.multiple_of((y + d) % 4 * 64, 64), 64)], cross_y.at[d],
            cy_s.at[d], cy_r.at[d], at_y(d),
        )

    for d in range(1, 4):
        cross_y_copy(d).start()

    for d in range(1, 4):
        gram_y_copy(d).wait_recv()
    gram_za[zl] = gram_part[eight(y), :] + gram_y[1] + gram_y[2] + gram_y[3]

    def gram_za_copy(d):
        return remote(
            gram_za.at[zl], gram_za.at[zl], ga_s.at[d], ga_r.at[d],
            ((zh * 4 + (zl + d) % 4) * 4 + y, col),
        )

    def gram_za_recv(d):
        return remote(
            gram_za.at[zl], gram_za.at[(zl + 4 - d) % 4], ga_s.at[d], ga_r.at[d],
            ((zh * 4 + (zl + d) % 4) * 4 + y, col),
        )

    for d in range(1, 4):
        gram_za_copy(d).start()
    for d in range(1, 4):
        gram_za_recv(d).wait_recv()
    gram_zb[zh] = (gram_za[0] + gram_za[1]) + (gram_za[2] + gram_za[3])

    def gram_zb_copy(d, slot_of):
        return remote(
            gram_zb.at[zh], gram_zb.at[slot_of], gb_s.at[d], gb_r.at[d],
            ((((zh + d) % 4) * 4 + zl) * 4 + y, col),
        )

    for d in range(1, 4):
        gram_zb_copy(d, zh).start()

    for d in range(1, 4):
        cross_y_copy(d).wait_recv()
    own_rows = pl.ds(pl.multiple_of(y * 64, 64), 64)
    cross_s[...] = (cross_part[own_rows, :] + cross_y[1]) + (cross_y[2] + cross_y[3])

    def tile(ref, base, who):
        return ref.at[
            pl.ds(pl.multiple_of(base + who // 2 * 8, 8), 8),
            pl.ds(pl.multiple_of(who % 2 * LANES, LANES), LANES),
        ]

    def cross_z_copy(d):
        return remote(
            tile(cross_s, 0, (z + d) % 16), cross_z.at[d], cz_s.at[d], cz_r.at[d], at_z(d)
        )

    @pl.loop(1, 16)
    def _(d):
        cross_z_copy(d).start()

    for d in range(1, 4):
        gram_zb_copy(d, (zh + 4 - d) % 4).wait_recv()
    gram_full[eight(col * 4 + y), :] = (gram_zb[0] + gram_zb[1]) + (gram_zb[2] + gram_zb[3])

    def gram_f_copy(d, who):
        block = gram_full.at[eight(who)]
        return remote(gram_full.at[eight(col * 4 + y)], block, gf_s.at[d], gf_r.at[d], at_plane(d))

    @pl.loop(1, 32)
    def _(d):
        gram_f_copy(d, col * 4 + y).start()

    @pl.loop(1, 16)
    def _(d):
        cross_z_copy(d).wait_recv()

    mine_s = pl.ds(pl.multiple_of(z // 2 * 8, 8), 8)
    mine_l = pl.ds(pl.multiple_of(z % 2 * LANES, LANES), LANES)
    total = cross_s[mine_s, mine_l]
    for d in range(1, 16):
        total = total + cross_z[d]
    cross_full[pl.ds(pl.multiple_of(y * 64 + z // 2 * 8, 8), 8), mine_l] = total

    def cross_g_copy(d, who):
        return remote(
            tile(cross_full, y * 64, z), tile(cross_full, y * 64, who), cg_s.at[d], cg_r.at[d], at_z(d)
        )

    @pl.loop(1, 16)
    def _(d):
        cross_g_copy(d, z).start()

    @pl.loop(1, 32)
    def _(d):
        spot = (y * 8 + col + 32 - d) % 32
        gram_f_copy(d, spot % 8 * 4 + spot // 8).wait_recv()

    gram_out[...] = gram_full[...]

    @pl.loop(1, 16)
    def _(d):
        cross_g_copy(d, (z + 16 - d) % 16).wait_recv()

    def cross_f_copy(d, who):
        return remote(
            cross_full.at[own_rows], cross_full.at[pl.ds(pl.multiple_of(who * 64, 64), 64)],
            cf_s.at[d], cf_r.at[d], at_y(d),
        )

    for d in range(1, 4):
        cross_f_copy(d, y).start()
    for d in range(1, 4):
        cross_f_copy(d, (y + 4 - d) % 4).wait_recv()
    cross_out[...] = cross_full[...]

    keep.wait()
    for i in range(6):
        sends[i].wait_send()
    for i in range(8):
        to_twin[i].wait_send()
    for d in range(1, 4):
        gram_y_copy(d).wait_send()
        gram_za_copy(d).wait_send()
        gram_zb_copy(d, zh).wait_send()
        cross_y_copy(d).wait_send()
        cross_f_copy(d, y).wait_send()

    @pl.loop(1, 16)
    def _(d):
        cross_z_copy(d).wait_send()
        cross_g_copy(d, z).wait_send()

    @pl.loop(1, 32)
    def _(d):
        gram_f_copy(d, col * 4 + y).wait_send()


def factor_block(work, lower, index):
    order = work.shape[0]
    start = index * STEP
    upper_half = start < LANES
    places = [(work, 0), (work, 1), (lower, 0)] if upper_half else [(work, 1), (lower, 0), (lower, 1)]
    rows = [ref[start : start + STEP, LANES * q : LANES * (q + 1)] for ref, q in places]
    lane = start % LANES
    down = lax.broadcasted_iota(jnp.int32, (STEP, LANES), 0)
    columns = [jnp.broadcast_to(rows[0][:, lane + j : lane + j + 1], (STEP, LANES)) for j in range(STEP)]
    for j in range(STEP):
        scale = lax.rsqrt(columns[j][j : j + 1, :])
        below = jnp.where(down > j, columns[j] * scale, 0.0)
        for m in range(j + 1, STEP):
            columns[m] = columns[m] - below * below[m : m + 1, :]
        for q in range(3):
            pivot_row = rows[q][j : j + 1, :] * scale
            rows[q] = jnp.where(down == j, pivot_row, rows[q] - below * pivot_row)
    for (ref, q), value in zip(places, rows):
        ref[start : start + STEP, LANES * q : LANES * (q + 1)] = value
    if start + STEP < order:
        if upper_half:
            left = jnp.concatenate([rows[0], rows[1]], 1)[:, start + STEP :]
        else:
            left = rows[0][:, start + STEP - LANES :]
        update = lax.dot_general(
            left, jnp.concatenate(rows, 1), (((0,), (0,)), ((), ())),
            precision=HIGHEST, preferred_element_type=F32,
        )
        for i, (ref, q) in enumerate(places):
            ref[start + STEP :, LANES * q : LANES * (q + 1)] -= update[:, LANES * i : LANES * (i + 1)]


def solve_kernel(gram, cross, factor_out, coupling_out, solved_out, work, lower):
    order = gram.shape[0]
    across = lax.broadcasted_iota(jnp.int32, (order, order), 1)
    down = lax.broadcasted_iota(jnp.int32, (order, order), 0)
    work[...] = gram[...]
    lower[...] = jnp.where(down == across, 1.0, 0.0)
    for index in range(order // STEP):
        factor_block(work, lower, index)
    coupling = jnp.dot(lower[...], cross[...], precision=HIGHEST, preferred_element_type=F32)
    coupling_out[...] = coupling
    solved_out[...] = lax.dot_general(
        lower[...], coupling, (((0,), (0,)), ((), ())), precision=HIGHEST, preferred_element_type=F32
    )
    work[...] = jnp.where(across >= down, work[...], 0.0).T
    width = factor_out.shape[0]
    col = lax.axis_index("col")
    factor_out[...] = work[pl.ds(pl.multiple_of(col * width, width), width), :]


def reduce_call(pt, trailing):
    dma = pltpu.SemaphoreType.DMA
    rows = pt.shape[1]
    square = jax.ShapeDtypeStruct((256, 256), F32)
    vmem = pl.BlockSpec(memory_space=pltpu.VMEM)
    hbm = pl.BlockSpec(memory_space=pl.ANY)
    return pl.pallas_call(
        reduce_kernel,
        out_shape=(jax.ShapeDtypeStruct((256, rows), F32), square, square),
        in_specs=[hbm, hbm],
        out_specs=(hbm, vmem, vmem),
        scratch_shapes=[
            pltpu.VMEM((256, rows), F32),
            pltpu.VMEM(trailing.shape, F32),
            pltpu.VMEM((32, 256), F32),
            pltpu.VMEM((4, 8, 256), F32),
            pltpu.VMEM((4, 8, 256), F32),
            pltpu.VMEM((4, 8, 256), F32),
            pltpu.VMEM((256, 256), F32),
            pltpu.VMEM((256, 256), F32),
            pltpu.VMEM((4, 64, 256), F32),
            pltpu.VMEM((64, 256), F32),
            pltpu.VMEM((16, 8, LANES), F32),
            pltpu.VMEM((256, 256), F32),
            dma((3,)),
            dma((6,)), dma((6,)), dma((8,)), dma((8,)),
            dma((4,)), dma((4,)), dma((4,)), dma((4,)), dma((4,)), dma((4,)),
            dma((32,)), dma((32,)),
            dma((4,)), dma((4,)), dma((16,)), dma((16,)), dma((16,)), dma((16,)), dma((4,)), dma((4,)),
        ],
        compiler_params=pltpu.CompilerParams(
            collective_id=0, has_side_effects=True, vmem_limit_bytes=40 * 2**20
        ),
    )(pt, trailing)


def solve_call(gram, cross):
    square = jax.ShapeDtypeStruct((256, 256), F32)
    return pl.pallas_call(
        solve_kernel,
        out_shape=(jax.ShapeDtypeStruct((32, 256), F32), square, square),
        scratch_shapes=[pltpu.VMEM((256, 256), F32), pltpu.VMEM((256, 256), F32)],
        compiler_params=pltpu.CompilerParams(vmem_limit_bytes=16 * 2**20),
    )(gram, cross)


def on_device(panel, trailing):
    whole_t, gram, cross = reduce_call(panel.T, trailing)
    factor_t, coupling, solved = solve_call(gram, cross)
    updated = trailing - jnp.dot(
        whole_t.T, solved, precision=lax.Precision.HIGH, preferred_element_type=F32
    )
    return factor_t.T, coupling, updated


def solution(mesh):
    in_specs = (P("row", "col"), P("row", "col"))
    out_specs = (P(None, "col"), P(None, "col"), P("row", "col"))
    return jax.shard_map(
        on_device, mesh=mesh, in_specs=in_specs, out_specs=out_specs, check_vma=False
    )
```

time: 1870 us -> 80.4 us (0.04); the launches traced: 1840 us -> 80.2 us
  other arithmetic: 1270 us -> 0 us
  waiting for transfers between devices: 295 us -> 0 us
  loops' own time: 192 us -> 0 us
  Pallas kernels: 0 us -> 73.9 us
  matrix products: 63.5 us -> 3.15 us
    reduce_sum x1024 -> x0, other arithmetic: 611 us -> none  [the longest x256 272 us: column_step(): column = jnp.sum(work * pick[None, :], axis=1)]
    add x512 -> x0, other arithmetic: 480 us -> none  [the longest x256 452 us: column_step(): lower = lower + column[:, None] * pick[None, :]]
    psum x1 -> x0, waiting for transfers between devices: 253 us -> none  [on_device(): gram = lax.psum(gram_local, 'row')]
    another operation x2 -> x0, loops' own time: 192 us -> none  [the longest x1 181 us: upper_factor(): work, lower = lax.fori_loop(0, order, column_step, start)]
    div x256 -> x0, other arithmetic: 177 us -> none  [back_step(): fresh = (pick - known) / pivot]
    pallas_call x0 -> x2, Pallas kernels: none -> 73.9 us  [the longest x1 61.9 us: reduce_call(): pl.pallas_call(reduce_kernel, out_shape=(jax.ShapeDtypeStruct((256, rows)...]
    dot_general x261 -> x1, matrix products: 63.5 us -> 3.15 us  [on_device(): jnp.dot(whole_t.T, solved, precision=lax.Precision.HIGH, preferred_elemen...]
    all_gather x1 -> x0, waiting for transfers between devices: 40.8 us -> none  [on_device(): whole = lax.all_gather(panel, 'col', axis=1, tiled=True)]
  transfers between devices with their start and end apart: 2 -> 0, of which waited for: 2 -> 0; matrix products, arithmetic and copies ran while one was open for 0% -> 0% of each run, Pallas kernels for 0% -> 0%
where the time goes in v1:
time: 80.4 us; the launch traced here: 80.2 us
  Pallas kernels  73.9 us (92%)
  matrix products  3.15 us (4%)
  local copies, waits for them, and re-layouts  2.53 us (3%)
    pallas_call x1, Pallas kernels, reduce_call(): pl.pallas_call(reduce_kernel, out_shape=(jax.ShapeDtypeStruct((256, rows)...  61.9 us
    pallas_call x1, Pallas kernels, solve_call(): pl.pallas_call(solve_kernel, out_shape=(jax.ShapeDtypeStruct((32, 256), F...  12 us
    dot_general x1, matrix products, on_device(): jnp.dot(whole_t.T, solved, precision=lax.Precision.HIGH, preferred_elemen...  3.15 us
    unnamed x4, local copies, waits for them, and re-layouts  2.53 us

profile of v1, /device:TPU:1, one launch (start us, length us, event | category | flops | bytes accessed | tf_op | source)
XLA Modules:
  0.0 80.2 jit_solution(11397197767690842837)
XLA Ops:
  0.6 0.0 copy-start
  0.6 1.6 %copy-done = f32[2048,256]{1,0:T(8,128)S(1)} copy-done((f32[2048,256]{1,0:T(8,128)S(1)}, f32[2048,256]{1,0:T(8,128)}, u32[]{:S(2)}) %copy-start) | copy-done | bytes 2097176
  2.2 0.0 copy-start.1
  2.2 0.9 %copy-done.1 = f32[2048,32]{0,1:T(8,128)S(1)} copy-done((f32[2048,32]{0,1:T(8,128)S(1)}, f32[2048,32]{0,1:T(8,128)}, u32[]{:S(2)}) %copy-start.1) | copy-done | bytes 262168
  3.2 61.9 %shard_map.49 = (f32[256,2048]{1,0:T(8,128)S(1)}, f32[256,256]{1,0:T(8,128)S(1)}, f32[256,256]{1,0:T(8,128)S(1)}) custom-call(f32[32,2048]{1,0:T(8,128)S(1)} %bitcast.4, f32[2048,256]{1,0:T(8,128)S(1)} %copy-done), custom_call_target="tpu_custom_call" | custom-call | tf_op jit(solution)/shard_map/pallas_call | solution.py:348
  65.1 12.0 %shard_map.50 = (f32[32,256]{1,0:T(8,128)}, f32[256,256]{1,0:T(8,128)}, f32[256,256]{1,0:T(8,128)S(1)}) custom-call(f32[256,256]{1,0:T(8,128)S(1)} %get-tuple-element.9.gram, f32[256,256]{1,0:T(8,128)S(1)} %get-tuple-element.10.cross), custom_call_target="tpu_custom_call" | custom-call | tf_op jit(solution)/shard_map/pallas_call | solution.py:380
  77.1 3.2 %convolution_subtract_fusion = f32[2048,256]{1,0:T(8,128)} fusion(f32[2048,256]{1,0:T(8,128)S(1)} %copy-done, f32[256,2048]{1,0:T(8,128)S(1)} %get-tuple-element.13, f32[256,256]{1,0:T(8,128)S(1)} %get-tuple-element.14), kind=kOutput, calls=%fused_computation | convolution fusion | flops 805830656 | bytes 6553600 | tf_op jit(solution)/shard_map/dot_general | solution.py:391
Async XLA Ops:
  0.6 1.6 %copy-start = (f32[2048,256]{1,0:T(8,128)S(1)}, f32[2048,256]{1,0:T(8,128)}, u32[]{:S(2)}) copy-start(f32[2048,256]{1,0:T(8,128)} %tr.1) | copy-start | bytes 6291460
  2.2 0.9 %copy-start.1 = (f32[2048,32]{0,1:T(8,128)S(1)}, f32[2048,32]{0,1:T(8,128)}, u32[]{:S(2)}) copy-start(f32[2048,32]{0,1:T(8,128)} %param.2) | copy-start | bytes 786436

commit v2 on v1

v2 whole, which is shorter than its diff:
```python
import functools

import jax
import jax.numpy as jnp
from jax import lax
from jax.experimental import pallas as pl
from jax.experimental.pallas import tpu as pltpu
from jax.sharding import PartitionSpec as P

F32 = jnp.float32
BF16 = jnp.bfloat16
HIGHEST = lax.Precision.HIGHEST
MESH = pl.DeviceIdType.MESH
STEP = 16
LANES = 128


def split(value):
    high = value.astype(BF16)
    low = (value - high.astype(F32)).astype(BF16)
    return high, low


def dot3(left, right, dims):
    left_hi, left_lo = split(left)
    right_hi, right_lo = split(right)
    dot = functools.partial(
        lax.dot_general, dimension_numbers=(dims, ((), ())), preferred_element_type=F32
    )
    return dot(left_hi, right_hi) + (dot(left_hi, right_lo) + dot(left_lo, right_hi))


def remote(src, dst, send, recv, where):
    return pltpu.make_async_remote_copy(
        src_ref=src, dst_ref=dst, send_sem=send, recv_sem=recv, device_id=where, device_id_type=MESH
    )


def total_of(parts):
    while len(parts) > 1:
        parts = [sum(parts[i : i + 2][1:], parts[i]) for i in range(0, len(parts), 2)]
    return parts[0]


def at(start, size):
    return pl.ds(pl.multiple_of(start * size, size), size)


def panel_kernel(
    pt, tr, whole_out, factor_out, coupling_out, solved_out,
    whole, trail, gram_part, gram_y, gram_z, gram_full,
    cross_part, cross_g, cross_z, cross_full, lower,
    loc_sem, px_s, px_r, sb_s, sb_r, gy_s, gy_r, gz_s, gz_r, gf_s, gf_r,
    cg_s, cg_r, cz_s, cz_r, cf_s, cf_r,
):
    row, col = lax.axis_index("row"), lax.axis_index("col")
    rem, div = lax.rem, lax.div
    z, y = div(row, 4), rem(row, 4)
    x, core = div(col, 2), rem(col, 2)
    zh, zl = div(z, 4), rem(z, 4)
    group = y * 4 + zl

    def at_y(d):
        return (z * 4 + rem(y + d, 4), col)

    def at_z(d):
        return (rem(z + d, 16) * 4 + y, col)

    def at_group(d):
        spot = rem(group + d, 16)
        return (zh * 16 + rem(spot, 4) * 4 + div(spot, 4), col)

    def at_plane(d):
        spot = rem(y * 8 + col + d, 32)
        return (z * 4 + div(spot, 8), rem(spot, 8))

    barrier = pltpu.get_barrier_semaphore()

    @pl.loop(1, 32)
    def _(d):
        pl.semaphore_signal(barrier, inc=1, device_id=at_plane(d), device_id_type=MESH)

    for d in range(1, 16):
        pl.semaphore_signal(barrier, inc=1, device_id=at_z(d), device_id_type=MESH)
    for dy in range(1, 4):
        for dz in range(1, 4):
            where = (zh * 16 + rem(zl + dz, 4) * 4 + rem(y + dy, 4), col)
            pl.semaphore_signal(barrier, inc=1, device_id=where, device_id_type=MESH)
    pl.semaphore_wait(barrier, 55)

    half = pt.shape[1] // 2
    right, left = (row, rem(x + 1, 4) * 2 + core), (row, rem(x + 3, 4) * 2 + core)
    twin = (row, x * 2 + 1 - core)

    def slot(far, part):
        return whole.at[at(rem(x + far, 4) * 2 + core, 32), pl.ds(part * half, half)]

    def own(part):
        return pt.at[:, pl.ds(part * half, half)]

    sends = {
        0: remote(own(0), slot(0, 0), px_s.at[0], px_r.at[0], right),
        1: remote(own(1), slot(0, 1), px_s.at[1], px_r.at[1], left),
        2: remote(own(1), slot(0, 1), px_s.at[2], px_r.at[2], right),
        3: remote(own(0), slot(0, 0), px_s.at[3], px_r.at[3], left),
    }
    for i in range(4):
        sends[i].start()
    to_twin = {}

    def relay(i, far, part, src=None):
        to_twin[i] = remote(
            slot(far, part) if src is None else src, slot(far, part), sb_s.at[i], sb_r.at[i], twin
        )
        to_twin[i].start()

    relay(6, 0, 0, own(0))
    relay(7, 0, 1, own(1))
    mine = pltpu.make_async_copy(pt, whole.at[at(col, 32), :], loc_sem.at[0])
    mine.start()
    load = pltpu.make_async_copy(tr, trail, loc_sem.at[1])
    load.start()

    sends[0].wait_recv()
    sends[4] = remote(slot(3, 0), slot(3, 0), px_s.at[4], px_r.at[4], right)
    sends[4].start()
    relay(0, 3, 0)
    sends[1].wait_recv()
    sends[5] = remote(slot(1, 1), slot(1, 1), px_s.at[5], px_r.at[5], left)
    sends[5].start()
    relay(1, 1, 1)
    sends[2].wait_recv()
    relay(2, 3, 1)
    sends[3].wait_recv()
    relay(3, 1, 0)
    sends[4].wait_recv()
    relay(4, 2, 0)
    sends[5].wait_recv()
    relay(5, 2, 1)
    mine.wait()
    load.wait()
    for i in range(8):
        to_twin[i].wait_recv()

    gram_part[...] = lax.dot_general(
        whole[at(col, 32), :], whole[...],
        (((1,), (1,)), ((), ())), precision=HIGHEST, preferred_element_type=F32,
    )

    def gram_y_copy(d):
        return remote(gram_part.at[at(rem(y + d, 4), 8)], gram_y.at[d], gy_s.at[d], gy_r.at[d], at_y(d))

    for d in (2, 1, 3):
        gram_y_copy(d).start()

    keep = pltpu.make_async_copy(whole, whole_out, loc_sem.at[2])
    keep.start()
    chunk = 512
    cross_part[...] = jnp.zeros_like(cross_part)

    @pl.loop(0, pt.shape[1] // chunk)
    def _(i):
        cross_part[...] += dot3(whole[:, at(i, chunk)], trail[at(i, chunk), :], ((1,), (0,)))

    def cross_g_copy(d):
        return remote(
            cross_part.at[at(rem(group + d, 16), 16)], cross_g.at[d], cg_s.at[d], cg_r.at[d], at_group(d)
        )

    @pl.loop(1, 16)
    def _(d):
        cross_g_copy(d).start()

    for d in range(1, 4):
        gram_y_copy(d).wait_recv()
    gram_z[z] = (gram_part[at(y, 8), :] + gram_y[1]) + (gram_y[2] + gram_y[3])

    def gram_z_copy(d, who):
        return remote(gram_z.at[z], gram_z.at[who], gz_s.at[d], gz_r.at[d], at_z(d))

    for d in (8, 7, 9, 6, 10, 5, 11, 4, 12, 3, 13, 2, 14, 1, 15):
        gram_z_copy(d, z).start()

    @pl.loop(1, 16)
    def _(d):
        cross_g_copy(d).wait_recv()

    cross_z[zh] = total_of([cross_part[at(group, 16), :]] + [cross_g[d] for d in range(1, 16)])

    def cross_z_copy(d, who):
        where = (rem(z + 4 * d, 16) * 4 + y, col)
        return remote(cross_z.at[zh], cross_z.at[who], cz_s.at[d], cz_r.at[d], where)

    for d in (2, 1, 3):
        cross_z_copy(d, zh).start()

    for d in range(1, 16):
        gram_z_copy(d, rem(z + 16 - d, 16)).wait_recv()
    gram_full[at(col * 4 + y, 8), :] = total_of([gram_z[i] for i in range(16)])

    def gram_f_copy(d, who):
        return remote(
            gram_full.at[at(col * 4 + y, 8)], gram_full.at[at(who, 8)], gf_s.at[d], gf_r.at[d], at_plane(d)
        )

    @pl.loop(1, 32)
    def _(d):
        gram_f_copy(d, col * 4 + y).start()

    for d in range(1, 4):
        cross_z_copy(d, rem(zh + 4 - d, 4)).wait_recv()
    cross_full[at(group, 16), :] = total_of([cross_z[i] for i in range(4)])

    def cross_f_copy(d, who):
        return remote(
            cross_full.at[at(group, 16)], cross_full.at[at(who, 16)], cf_s.at[d], cf_r.at[d], at_group(d)
        )

    @pl.loop(1, 16)
    def _(d):
        cross_f_copy(d, group).start()

    @pl.loop(1, 32)
    def _(d):
        spot = rem(y * 8 + col + 32 - d, 32)
        gram_f_copy(d, rem(spot, 8) * 4 + div(spot, 8)).wait_recv()

    @pl.loop(1, 32)
    def _(d):
        gram_f_copy(d, col * 4 + y).wait_send()

    order = gram_full.shape[0]
    across = lax.broadcasted_iota(jnp.int32, (order, order), 1)
    down = lax.broadcasted_iota(jnp.int32, (order, order), 0)
    lower[...] = jnp.where(down == across, 1.0, 0.0)
    for index in range(order // STEP):
        factor_block(gram_full, lower, index)

    @pl.loop(1, 16)
    def _(d):
        cross_f_copy(d, rem(group + 16 - d, 16)).wait_recv()

    coupling = jnp.dot(lower[...], cross_full[...], precision=HIGHEST, preferred_element_type=F32)
    coupling_out[...] = coupling
    solved_out[...] = lax.dot_general(
        lower[...], coupling, (((0,), (0,)), ((), ())), precision=HIGHEST, preferred_element_type=F32
    )
    gram_full[...] = jnp.where(across >= down, gram_full[...], 0.0).T
    factor_out[...] = gram_full[at(col, 32), :]

    keep.wait()
    for i in range(6):
        sends[i].wait_send()
    for i in range(8):
        to_twin[i].wait_send()
    for d in range(1, 4):
        gram_y_copy(d).wait_send()
        cross_z_copy(d, zh).wait_send()

    @pl.loop(1, 16)
    def _(d):
        gram_z_copy(d, z).wait_send()
        cross_g_copy(d).wait_send()
        cross_f_copy(d, group).wait_send()


def factor_block(work, lower, index):
    order = work.shape[0]
    start = index * STEP
    upper_half = start < LANES
    places = [(work, 0), (work, 1), (lower, 0)] if upper_half else [(work, 1), (lower, 0), (lower, 1)]
    rows = jnp.concatenate([ref[start : start + STEP, LANES * q : LANES * (q + 1)] for ref, q in places], 1)
    lane = start % LANES
    down = lax.broadcasted_iota(jnp.int32, (STEP, LANES), 0)
    wide = lax.broadcasted_iota(jnp.int32, rows.shape, 0)
    columns = [jnp.broadcast_to(rows[:, lane + j : lane + j + 1], (STEP, LANES)) for j in range(STEP)]
    for j in range(STEP):
        scale = lax.rsqrt(columns[j][j : j + 1, :])
        below = jnp.where(down > j, columns[j] * scale, 0.0)
        for m in range(j + 1, STEP):
            columns[m] = columns[m] - below * below[m : m + 1, :]
        pivot_row = rows[j : j + 1, :] * jnp.concatenate([scale] * 3, 1)
        rows = jnp.where(wide == j, pivot_row, rows - jnp.concatenate([below] * 3, 1) * pivot_row)
    for i, (ref, q) in enumerate(places):
        ref[start : start + STEP, LANES * q : LANES * (q + 1)] = rows[:, LANES * i : LANES * (i + 1)]
    if start + STEP < order:
        left = rows[:, start + STEP : 2 * LANES] if upper_half else rows[:, start + STEP - LANES : LANES]
        update = lax.dot_general(
            left, rows, (((0,), (0,)), ((), ())), precision=HIGHEST, preferred_element_type=F32
        )
        for i, (ref, q) in enumerate(places):
            ref[start + STEP :, LANES * q : LANES * (q + 1)] -= update[:, LANES * i : LANES * (i + 1)]


def panel_call(pt, trailing):
    dma = pltpu.SemaphoreType.DMA
    rows = pt.shape[1]
    square = jax.ShapeDtypeStruct((256, 256), F32)
    vmem = pl.BlockSpec(memory_space=pltpu.VMEM)
    hbm = pl.BlockSpec(memory_space=pltpu.HBM)
    return pl.pallas_call(
        panel_kernel,
        out_shape=(
            jax.ShapeDtypeStruct((256, rows), F32), jax.ShapeDtypeStruct((32, 256), F32), square, square,
        ),
        in_specs=[hbm, hbm],
        out_specs=(pl.BlockSpec(memory_space=pl.ANY), vmem, vmem, vmem),
        scratch_shapes=[
            pltpu.VMEM((256, rows), F32),
            pltpu.VMEM(trailing.shape, F32),
            pltpu.VMEM((32, 256), F32),
            pltpu.VMEM((4, 8, 256), F32),
            pltpu.VMEM((16, 8, 256), F32),
            pltpu.VMEM((256, 256), F32),
            pltpu.VMEM((256, 256), F32),
            pltpu.VMEM((16, 16, 256), F32),
            pltpu.VMEM((4, 16, 256), F32),
            pltpu.VMEM((256, 256), F32),
            pltpu.VMEM((256, 256), F32),
            dma((3,)),
            dma((6,)), dma((6,)), dma((8,)), dma((8,)),
            dma((4,)), dma((4,)), dma((16,)), dma((16,)), dma((32,)), dma((32,)),
            dma((16,)), dma((16,)), dma((4,)), dma((4,)), dma((16,)), dma((16,)),
        ],
        compiler_params=pltpu.CompilerParams(
            collective_id=0, has_side_effects=True, vmem_limit_bytes=40 * 2**20
        ),
    )(pltpu.with_memory_space_constraint(pt, pltpu.HBM), pltpu.with_memory_space_constraint(trailing, pltpu.HBM))


def on_device(panel, trailing):
    whole_t, factor_t, coupling, solved = panel_call(panel.T, trailing)
    updated = trailing - jnp.dot(
        whole_t.T, solved, precision=lax.Precision.HIGH, preferred_element_type=F32
    )
    return factor_t.T, coupling, updated


def solution(mesh):
    in_specs = (P("row", "col"), P("row", "col"))
    out_specs = (P(None, "col"), P(None, "col"), P("row", "col"))
    return jax.shard_map(
        on_device, mesh=mesh, in_specs=in_specs, out_specs=out_specs, check_vma=False
    )
```

time: 80.4 us -> 75.1 us (0.934)
  Pallas kernels: 73.9 us -> 69.8 us
  local copies, waits for them, and re-layouts: 2.53 us -> 1.32 us
    pallas_call x2 -> x1, Pallas kernels: 73.9 us -> 69.8 us  [panel_call(): pl.pallas_call(panel_kernel, out_shape=(jax.ShapeDtypeStruct((256, rows),...]
    unnamed x4, local copies, waits for them, and re-layouts: 2.53 us -> 1.32 us
where the time goes in v2:
time: 75.1 us; the launch traced here: 75 us
  Pallas kernels  69.8 us (93%)
  matrix products  3.15 us (4%)
  local copies, waits for them, and re-layouts  1.32 us (2%)
    pallas_call x1, Pallas kernels, panel_call(): pl.pallas_call(panel_kernel, out_shape=(jax.ShapeDtypeStruct((256, rows),...  69.8 us
    dot_general x1, matrix products, on_device(): jnp.dot(whole_t.T, solved, precision=lax.Precision.HIGH, preferred_elemen...  3.15 us

profile of v2, /device:TPU:1, one launch (start us, length us, event | category | flops | bytes accessed | tf_op | source)
XLA Modules:
  0.0 75.0 jit_solution(3510460773394950359)
XLA Ops:
  0.6 0.0 copy-start
  0.6 69.8 %shard_map.49 = (f32[256,2048]{1,0:T(8,128)S(1)}, f32[32,256]{1,0:T(8,128)S(1)}, f32[256,256]{1,0:T(8,128)S(1)}, f32[256,256]{1,0:T(8,128)S(1)}) custom-call(f32[32,2048]{1,0:T(8,128)} %bitcast.5, f32[2048,256]{1,0:T(8,128)} %tr.1), custom_call_target="tpu_custom_call" | custom-call | tf_op jit(solution)/shard_map/pallas_call | solution.py:301
  70.5 0.0 copy-done
  70.5 3.1 %convolution_subtract_fusion = f32[2048,256]{1,0:T(8,128)} fusion(f32[2048,256]{1,0:T(8,128)S(1)} %copy-done, f32[256,2048]{1,0:T(8,128)S(1)} %get-tuple-element.9, f32[256,256]{1,0:T(8,128)S(1)} %get-tuple-element.10), kind=kOutput, calls=%fused_computation | convolution fusion | flops 805830656 | bytes 6553600 | tf_op jit(solution)/shard_map/dot_general | solution.py:333
  73.6 0.6 copy.7
  74.3 0.7 copy.8
Async XLA Ops:
  0.6 69.9 %copy-start = (f32[2048,256]{1,0:T(8,128)S(1)}, f32[2048,256]{1,0:T(8,128)}, u32[]{:S(2)}) copy-start(f32[2048,256]{1,0:T(8,128)} %tr.1) | copy-start | bytes 6291460

commit v3 on v2

--- a/solution.py
+++ b/solution.py
@@ -47,10 +47,10 @@
 
 
 def panel_kernel(
-    pt, tr, whole_out, factor_out, coupling_out, solved_out,
-    whole, trail, gram_part, gram_y, gram_z, gram_full,
+    pt, tr, whole_out, upper_out, lower_out, cross_out,
+    whole, trail, slab, gram_part, gram_p, gram_z, gram_full,
     cross_part, cross_g, cross_z, cross_full, lower,
-    loc_sem, px_s, px_r, sb_s, sb_r, gy_s, gy_r, gz_s, gz_r, gf_s, gf_r,
+    loc_sem, ps_s, ps_r, px_s, px_r, sb_s, sb_r, gp_s, gp_r, gz_s, gz_r, gf_s, gf_r,
     cg_s, cg_r, cz_s, cz_r, cf_s, cf_r,
 ):
     row, col = lax.axis_index("row"), lax.axis_index("col")
@@ -60,9 +60,6 @@
     zh, zl = div(z, 4), rem(z, 4)
     group = y * 4 + zl
 
-    def at_y(d):
-        return (z * 4 + rem(y + d, 4), col)
-
     def at_z(d):
         return (rem(z + d, 16) * 4 + y, col)
 
@@ -70,23 +67,41 @@
         spot = rem(group + d, 16)
         return (zh * 16 + rem(spot, 4) * 4 + div(spot, 4), col)
 
+    mine = y * 8 + col
+
     def at_plane(d):
-        spot = rem(y * 8 + col + d, 32)
+        spot = rem(mine + d, 32)
         return (z * 4 + div(spot, 8), rem(spot, 8))
 
+    far_first = (8, 7, 9, 6, 10, 5, 11, 4, 12, 3, 13, 2, 14, 1, 15)
     barrier = pltpu.get_barrier_semaphore()
-
-    @pl.loop(1, 32)
-    def _(d):
-        pl.semaphore_signal(barrier, inc=1, device_id=at_plane(d), device_id_type=MESH)
-
-    for d in range(1, 16):
+    for d in far_first:
         pl.semaphore_signal(barrier, inc=1, device_id=at_z(d), device_id_type=MESH)
     for dy in range(1, 4):
         for dz in range(1, 4):
             where = (zh * 16 + rem(zl + dz, 4) * 4 + rem(y + dy, 4), col)
             pl.semaphore_signal(barrier, inc=1, device_id=where, device_id_type=MESH)
+
+    @pl.loop(1, 32)
+    def _(d):
+        pl.semaphore_signal(barrier, inc=1, device_id=at_plane(d), device_id_type=MESH)
+
     pl.semaphore_wait(barrier, 55)
+
+    def slab_copy(d):
+        who = rem(col + d, 8)
+        return remote(pt.at[:, at(who, 256)], slab.at[at(col, 32)], ps_s.at[d], ps_r.at[d], (row, who))
+
+    def slab_recv(d):
+        who = rem(col + d, 8)
+        return remote(
+            pt.at[:, at(who, 256)], slab.at[at(rem(col + 8 - d, 8), 32)], ps_s.at[d], ps_r.at[d], (row, who)
+        )
+
+    for d in (4, 3, 5, 2, 6, 1, 7):
+        slab_copy(d).start()
+    slab_own = pltpu.make_async_copy(pt.at[:, at(col, 256)], slab.at[at(col, 32)], loc_sem.at[3])
+    slab_own.start()
 
     half = pt.shape[1] // 2
     right, left = (row, rem(x + 1, 4) * 2 + core), (row, rem(x + 3, 4) * 2 + core)
@@ -116,10 +131,26 @@
 
     relay(6, 0, 0, own(0))
     relay(7, 0, 1, own(1))
-    mine = pltpu.make_async_copy(pt, whole.at[at(col, 32), :], loc_sem.at[0])
-    mine.start()
+    panel_own = pltpu.make_async_copy(pt, whole.at[at(col, 32), :], loc_sem.at[0])
+    panel_own.start()
     load = pltpu.make_async_copy(tr, trail, loc_sem.at[1])
     load.start()
+
+    slab_own.wait()
+    for d in range(1, 8):
+        slab_recv(d).wait_recv()
+    gram_part[...] = lax.dot_general(
+        slab[...], slab[...], (((1,), (1,)), ((), ())), precision=HIGHEST, preferred_element_type=F32
+    )
+
+    def gram_p_copy(d):
+        return remote(
+            gram_part.at[at(rem(mine + d, 32), 8)], gram_p.at[d], gp_s.at[d], gp_r.at[d], at_plane(d)
+        )
+
+    @pl.loop(1, 32)
+    def _(d):
+        gram_p_copy(d).start()
 
     sends[0].wait_recv()
     sends[4] = remote(slot(3, 0), slot(3, 0), px_s.at[4], px_r.at[4], right)
@@ -133,25 +164,27 @@
     relay(2, 3, 1)
     sends[3].wait_recv()
     relay(3, 1, 0)
+
+    @pl.loop(1, 32)
+    def _(d):
+        gram_p_copy(d).wait_recv()
+
+    gram_z[z] = total_of([gram_part[at(mine, 8), :]] + [gram_p[d] for d in range(1, 32)])
+
+    def gram_z_copy(d, who):
+        return remote(gram_z.at[z], gram_z.at[who], gz_s.at[d], gz_r.at[d], at_z(d))
+
+    for d in far_first:
+        gram_z_copy(d, z).start()
+
     sends[4].wait_recv()
     relay(4, 2, 0)
     sends[5].wait_recv()
     relay(5, 2, 1)
-    mine.wait()
+    panel_own.wait()
     load.wait()
     for i in range(8):
         to_twin[i].wait_recv()
-
-    gram_part[...] = lax.dot_general(
-        whole[at(col, 32), :], whole[...],
-        (((1,), (1,)), ((), ())), precision=HIGHEST, preferred_element_type=F32,
-    )
-
-    def gram_y_copy(d):
-        return remote(gram_part.at[at(rem(y + d, 4), 8)], gram_y.at[d], gy_s.at[d], gy_r.at[d], at_y(d))
-
-    for d in (2, 1, 3):
-        gram_y_copy(d).start()
 
     keep = pltpu.make_async_copy(whole, whole_out, loc_sem.at[2])
     keep.start()
@@ -171,15 +204,18 @@
     def _(d):
         cross_g_copy(d).start()
 
-    for d in range(1, 4):
-        gram_y_copy(d).wait_recv()
-    gram_z[z] = (gram_part[at(y, 8), :] + gram_y[1]) + (gram_y[2] + gram_y[3])
-
-    def gram_z_copy(d, who):
-        return remote(gram_z.at[z], gram_z.at[who], gz_s.at[d], gz_r.at[d], at_z(d))
-
-    for d in (8, 7, 9, 6, 10, 5, 11, 4, 12, 3, 13, 2, 14, 1, 15):
-        gram_z_copy(d, z).start()
+    for d in range(1, 16):
+        gram_z_copy(d, rem(z + 16 - d, 16)).wait_recv()
+    gram_full[at(mine, 8), :] = total_of([gram_z[i] for i in range(16)])
+
+    def gram_f_copy(d, who):
+        return remote(
+            gram_full.at[at(mine, 8)], gram_full.at[at(who, 8)], gf_s.at[d], gf_r.at[d], at_plane(d)
+        )
+
+    @pl.loop(1, 32)
+    def _(d):
+        gram_f_copy(d, mine).start()
 
     @pl.loop(1, 16)
     def _(d):
@@ -194,59 +230,44 @@
     for d in (2, 1, 3):
         cross_z_copy(d, zh).start()
 
-    for d in range(1, 16):
-        gram_z_copy(d, rem(z + 16 - d, 16)).wait_recv()
-    gram_full[at(col * 4 + y, 8), :] = total_of([gram_z[i] for i in range(16)])
-
-    def gram_f_copy(d, who):
-        return remote(
-            gram_full.at[at(col * 4 + y, 8)], gram_full.at[at(who, 8)], gf_s.at[d], gf_r.at[d], at_plane(d)
-        )
-
-    @pl.loop(1, 32)
-    def _(d):
-        gram_f_copy(d, col * 4 + y).start()
-
-    for d in range(1, 4):
-        cross_z_copy(d, rem(zh + 4 - d, 4)).wait_recv()
-    cross_full[at(group, 16), :] = total_of([cross_z[i] for i in range(4)])
-
-    def cross_f_copy(d, who):
-        return remote(
-            cross_full.at[at(group, 16)], cross_full.at[at(who, 16)], cf_s.at[d], cf_r.at[d], at_group(d)
-        )
-
-    @pl.loop(1, 16)
-    def _(d):
-        cross_f_copy(d, group).start()
-
-    @pl.loop(1, 32)
-    def _(d):
-        spot = rem(y * 8 + col + 32 - d, 32)
-        gram_f_copy(d, rem(spot, 8) * 4 + div(spot, 8)).wait_recv()
-
-    @pl.loop(1, 32)
-    def _(d):
-        gram_f_copy(d, col * 4 + y).wait_send()
+    @pl.loop(1, 32)
+    def _(d):
+        gram_f_copy(d, rem(mine + 32 - d, 32)).wait_recv()
+
+    @pl.loop(1, 32)
+    def _(d):
+        gram_f_copy(d, mine).wait_send()
 
     order = gram_full.shape[0]
     across = lax.broadcasted_iota(jnp.int32, (order, order), 1)
     down = lax.broadcasted_iota(jnp.int32, (order, order), 0)
     lower[...] = jnp.where(down == across, 1.0, 0.0)
-    for index in range(order // STEP):
+    for index in range(order // STEP // 2):
         factor_block(gram_full, lower, index)
 
+    for d in range(1, 4):
+        cross_z_copy(d, rem(zh + 4 - d, 4)).wait_recv()
+    cross_full[at(group, 16), :] = total_of([cross_z[i] for i in range(4)])
+
+    def cross_f_copy(d, who):
+        return remote(
+            cross_full.at[at(group, 16)], cross_full.at[at(who, 16)], cf_s.at[d], cf_r.at[d], at_group(d)
+        )
+
     @pl.loop(1, 16)
     def _(d):
+        cross_f_copy(d, group).start()
+
+    for index in range(order // STEP // 2, order // STEP):
+        factor_block(gram_full, lower, index)
+
+    @pl.loop(1, 16)
+    def _(d):
         cross_f_copy(d, rem(group + 16 - d, 16)).wait_recv()
 
-    coupling = jnp.dot(lower[...], cross_full[...], precision=HIGHEST, preferred_element_type=F32)
-    coupling_out[...] = coupling
-    solved_out[...] = lax.dot_general(
-        lower[...], coupling, (((0,), (0,)), ((), ())), precision=HIGHEST, preferred_element_type=F32
-    )
-    gram_full[...] = jnp.where(across >= down, gram_full[...], 0.0).T
-    factor_out[...] = gram_full[at(col, 32), :]
+    upper_out[...] = gram_full[...]
+    lower_out[...] = lower[...]
+    cross_out[...] = cross_full[...]
 
     keep.wait()
     for i in range(6):
@@ -254,7 +275,6 @@
     for i in range(8):
         to_twin[i].wait_send()
     for d in range(1, 4):
-        gram_y_copy(d).wait_send()
         cross_z_copy(d, zh).wait_send()
 
     @pl.loop(1, 16)
@@ -262,6 +282,13 @@
         gram_z_copy(d, z).wait_send()
         cross_g_copy(d).wait_send()
         cross_f_copy(d, group).wait_send()
+
+    for d in range(1, 8):
+        slab_copy(d).wait_send()
+
+    @pl.loop(1, 32)
+    def _(d):
+        gram_p_copy(d).wait_send()
 
 
 def factor_block(work, lower, index):
@@ -301,15 +328,16 @@
     return pl.pallas_call(
         panel_kernel,
         out_shape=(
-            jax.ShapeDtypeStruct((256, rows), F32), jax.ShapeDtypeStruct((32, 256), F32), square, square,
+            jax.ShapeDtypeStruct((256, rows), F32), square, square, square,
         ),
         in_specs=[hbm, hbm],
         out_specs=(pl.BlockSpec(memory_space=pl.ANY), vmem, vmem, vmem),
         scratch_shapes=[
             pltpu.VMEM((256, rows), F32),
             pltpu.VMEM(trailing.shape, F32),
-            pltpu.VMEM((32, 256), F32),
-            pltpu.VMEM((4, 8, 256), F32),
+            pltpu.VMEM((256, 256), F32),
+            pltpu.VMEM((256, 256), F32),
+            pltpu.VMEM((32, 8, 256), F32),
             pltpu.VMEM((16, 8, 256), F32),
             pltpu.VMEM((256, 256), F32),
             pltpu.VMEM((256, 256), F32),
@@ -317,9 +345,9 @@
             pltpu.VMEM((4, 16, 256), F32),
             pltpu.VMEM((256, 256), F32),
             pltpu.VMEM((256, 256), F32),
-            dma((3,)),
+            dma((4,)), dma((8,)), dma((8,)),
             dma((6,)), dma((6,)), dma((8,)), dma((8,)),
-            dma((4,)), dma((4,)), dma((16,)), dma((16,)), dma((32,)), dma((32,)),
+            dma((32,)), dma((32,)), dma((16,)), dma((16,)), dma((32,)), dma((32,)),
             dma((16,)), dma((16,)), dma((4,)), dma((4,)), dma((16,)), dma((16,)),
         ],
         compiler_params=pltpu.CompilerParams(
@@ -328,11 +356,52 @@
     )(pltpu.with_memory_space_constraint(pt, pltpu.HBM), pltpu.with_memory_space_constraint(trailing, pltpu.HBM))
 
 
+def update_kernel(whole, upper, lower, cross, trail, factor_out, coupling_out, updated_out, scratch, block, sems):
+    order = upper.shape[0]
+    across = lax.broadcasted_iota(jnp.int32, (order, order), 1)
+    down = lax.broadcasted_iota(jnp.int32, (order, order), 0)
+    coupling = jnp.dot(lower[...], cross[...], precision=HIGHEST, preferred_element_type=F32)
+    coupling_out[...] = coupling
+    solved = lax.dot_general(
+        lower[...], coupling, (((0,), (0,)), ((), ())), precision=HIGHEST, preferred_element_type=F32
+    )
+    steps, size = block.shape[0], block.shape[1]
+    copies = []
+    for i in range(steps):
+        rows = slice(i * size, (i + 1) * size)
+        block[i] = trail[rows, :] - dot3(whole[:, rows], solved, ((0,), (0,)))
+        copies.append(pltpu.make_async_copy(block.at[i], updated_out.at[pl.ds(i * size, size)], sems.at[i]))
+        copies[-1].start()
+    scratch[...] = jnp.where(across >= down, upper[...], 0.0).T
+    factor_out[...] = scratch[at(lax.axis_index("col"), 32), :]
+    for copy in copies:
+        copy.wait()
+
+
+def update_call(whole_t, upper, lower, cross, trailing):
+    rows, width = trailing.shape
+    vmem = pl.BlockSpec(memory_space=pltpu.VMEM)
+    steps = 8
+    return pl.pallas_call(
+        update_kernel,
+        out_shape=(
+            jax.ShapeDtypeStruct((32, 256), F32), jax.ShapeDtypeStruct((256, width), F32),
+            jax.ShapeDtypeStruct((rows, width), F32),
+        ),
+        in_specs=[vmem] * 5,
+        out_specs=(vmem, vmem, pl.BlockSpec(memory_space=pl.ANY)),
+        scratch_shapes=[
+            pltpu.VMEM((256, 256), F32),
+            pltpu.VMEM((steps, rows // steps, width), F32),
+            pltpu.SemaphoreType.DMA((steps,)),
+        ],
+        compiler_params=pltpu.CompilerParams(vmem_limit_bytes=40 * 2**20),
+    )(whole_t, upper, lower, cross, trailing)
+
+
 def on_device(panel, trailing):
-    whole_t, factor_t, coupling, solved = panel_call(panel.T, trailing)
-    updated = trailing - jnp.dot(
-        whole_t.T, solved, precision=lax.Precision.HIGH, preferred_element_type=F32
-    )
+    whole_t, upper, lower, cross = panel_call(panel.T, trailing)
+    factor_t, coupling, updated = update_call(whole_t, upper, lower, cross, trailing)
     return factor_t.T, coupling, updated
 
 

time: 75.1 us -> 68.8 us (0.916)
  matrix products: 3.15 us -> 0 us
  Pallas kernels: 69.8 us -> 68 us
  local copies, waits for them, and re-layouts: 1.32 us -> 0.01 us
    pallas_call x1, Pallas kernels: 69.8 us -> 64.2 us  [panel_call(): pl.pallas_call(panel_kernel, out_shape=(jax.ShapeDtypeStruct((256, rows),...]
    pallas_call x0 -> x1, Pallas kernels: none -> 3.79 us  [update_call(): pl.pallas_call(update_kernel, out_shape=(jax.ShapeDtypeStruct((32, 256),...]
    dot_general x1 -> x0, matrix products: 3.15 us -> none  [on_device(): jnp.dot(whole_t.T, solved, precision=lax.Precision.HIGH, preferred_elemen...]
    unnamed x4 -> x2, local copies, waits for them, and re-layouts: 1.32 us -> 0.01 us
where the time goes in v3:
time: 68.8 us; the launch traced here: 68.6 us
  Pallas kernels  68 us (99%)
    pallas_call x1, Pallas kernels, panel_call(): pl.pallas_call(panel_kernel, out_shape=(jax.ShapeDtypeStruct((256, rows),...  64.2 us
    pallas_call x1, Pallas kernels, update_call(): pl.pallas_call(update_kernel, out_shape=(jax.ShapeDtypeStruct((32, 256),...  3.79 us

profile of v3, /device:TPU:1, one launch (start us, length us, event | category | flops | bytes accessed | tf_op | source)
XLA Modules:
  0.0 68.6 jit_solution(3524510732942536509)
XLA Ops:
  0.6 0.0 copy-start
  0.6 64.2 %shard_map.49 = (f32[256,2048]{1,0:T(8,128)S(1)}, f32[256,256]{1,0:T(8,128)S(1)}, f32[256,256]{1,0:T(8,128)S(1)}, f32[256,256]{1,0:T(8,128)S(1)}) custom-call(f32[32,2048]{1,0:T(8,128)} %bitcast.2, f32[2048,256]{1,0:T(8,128)} %trail.1), custom_call_target="tpu_custom_call" | custom-call | tf_op jit(solution)/shard_map/pallas_call | solution.py:328
  64.8 0.0 copy-done
  64.8 3.8 %shard_map.50 = (f32[32,256]{1,0:T(8,128)}, f32[256,256]{1,0:T(8,128)}, f32[2048,256]{1,0:T(8,128)}) custom-call(f32[256,2048]{1,0:T(8,128)S(1)} %get-tuple-element.10.whole, f32[256,256]{1,0:T(8,128)S(1)} %get-tuple-element.11.upper, f32[256,256]{1,0:T(8,128)S(1)} %get-tuple-element.12.lower, f32[256,256]{1,0:T(8,128)S(1)} %get-tuple-element.13.cross, ...), custom_call_target="tpu_custom_call" | custom-call | tf_op jit(solution)/shard_map/pallas_call | solution.py:385
Async XLA Ops:
  0.6 64.2 %copy-start = (f32[2048,256]{1,0:T(8,128)S(1)}, f32[2048,256]{1,0:T(8,128)}, u32[]{:S(2)}) copy-start(f32[2048,256]{1,0:T(8,128)} %trail.1) | copy-start | bytes 6291460

commit v4 on v3

--- a/solution.py
+++ b/solution.py
@@ -48,7 +48,7 @@
 
 def panel_kernel(
     pt, tr, whole_out, upper_out, lower_out, cross_out,
-    whole, trail, slab, gram_part, gram_p, gram_z, gram_full,
+    whole, trail, trail_hi, trail_lo, slab, gram_part, gram_p, gram_z, gram_full,
     cross_part, cross_g, cross_z, cross_full, lower,
     loc_sem, ps_s, ps_r, px_s, px_r, sb_s, sb_r, gp_s, gp_r, gz_s, gz_r, gf_s, gf_r,
     cg_s, cg_r, cz_s, cz_r, cf_s, cf_r,
@@ -58,57 +58,51 @@
     z, y = div(row, 4), rem(row, 4)
     x, core = div(col, 2), rem(col, 2)
     zh, zl = div(z, 4), rem(z, 4)
-    group = y * 4 + zl
+    ys = [y] + [rem(y + d, 4) for d in range(1, 4)]
+    cols = [col] + [rem(col + d, 8) for d in range(1, 8)]
+    zs = [z] + [rem(z + d, 16) for d in range(1, 16)]
+    near = [zl] + [rem(zl + d, 4) for d in range(1, 4)]
+    chips = [x] + [rem(x + d, 4) for d in range(1, 4)]
+
+    plane = [(dy, dc) for dy in (2, 1, 3, 0) for dc in (4, 3, 5, 2, 6, 1, 7, 0) if (dy, dc) != (0, 0)]
+    block = [(dy, dz) for dz in (2, 1, 3, 0) for dy in (2, 1, 3, 0) if (dy, dz) != (0, 0)]
+    line = (8, 7, 9, 6, 10, 5, 11, 4, 12, 3, 13, 2, 14, 1, 15)
+
+    def at_plane(dy, dc):
+        return (z * 4 + ys[dy], cols[dc])
 
     def at_z(d):
-        return (rem(z + d, 16) * 4 + y, col)
-
-    def at_group(d):
-        spot = rem(group + d, 16)
-        return (zh * 16 + rem(spot, 4) * 4 + div(spot, 4), col)
-
-    mine = y * 8 + col
-
-    def at_plane(d):
-        spot = rem(mine + d, 32)
-        return (z * 4 + div(spot, 8), rem(spot, 8))
-
-    far_first = (8, 7, 9, 6, 10, 5, 11, 4, 12, 3, 13, 2, 14, 1, 15)
+        return (zs[d] * 4 + y, col)
+
+    def at_block(dy, dz):
+        return (zh * 16 + near[dz] * 4 + ys[dy], col)
+
     barrier = pltpu.get_barrier_semaphore()
-    for d in far_first:
+    for d in line:
         pl.semaphore_signal(barrier, inc=1, device_id=at_z(d), device_id_type=MESH)
-    for dy in range(1, 4):
-        for dz in range(1, 4):
-            where = (zh * 16 + rem(zl + dz, 4) * 4 + rem(y + dy, 4), col)
-            pl.semaphore_signal(barrier, inc=1, device_id=where, device_id_type=MESH)
-
-    @pl.loop(1, 32)
-    def _(d):
-        pl.semaphore_signal(barrier, inc=1, device_id=at_plane(d), device_id_type=MESH)
-
+    for dy, dz in block:
+        if dy and dz:
+            pl.semaphore_signal(barrier, inc=1, device_id=at_block(dy, dz), device_id_type=MESH)
+    for dy, dc in plane:
+        pl.semaphore_signal(barrier, inc=1, device_id=at_plane(dy, dc), device_id_type=MESH)
     pl.semaphore_wait(barrier, 55)
 
-    def slab_copy(d):
-        who = rem(col + d, 8)
-        return remote(pt.at[:, at(who, 256)], slab.at[at(col, 32)], ps_s.at[d], ps_r.at[d], (row, who))
-
-    def slab_recv(d):
-        who = rem(col + d, 8)
+    def slab_copy(d, who):
         return remote(
-            pt.at[:, at(who, 256)], slab.at[at(rem(col + 8 - d, 8), 32)], ps_s.at[d], ps_r.at[d], (row, who)
+            pt.at[:, at(cols[d], 256)], slab.at[at(who, 32)], ps_s.at[d], ps_r.at[d], (row, cols[d])
         )
 
     for d in (4, 3, 5, 2, 6, 1, 7):
-        slab_copy(d).start()
+        slab_copy(d, col).start()
     slab_own = pltpu.make_async_copy(pt.at[:, at(col, 256)], slab.at[at(col, 32)], loc_sem.at[3])
     slab_own.start()
 
     half = pt.shape[1] // 2
-    right, left = (row, rem(x + 1, 4) * 2 + core), (row, rem(x + 3, 4) * 2 + core)
+    right, left = (row, chips[1] * 2 + core), (row, chips[3] * 2 + core)
     twin = (row, x * 2 + 1 - core)
 
     def slot(far, part):
-        return whole.at[at(rem(x + far, 4) * 2 + core, 32), pl.ds(part * half, half)]
+        return whole.at[at(chips[far] * 2 + core, 32), pl.ds(part * half, half)]
 
     def own(part):
         return pt.at[:, pl.ds(part * half, half)]
@@ -136,21 +130,31 @@
     load = pltpu.make_async_copy(tr, trail, loc_sem.at[1])
     load.start()
 
+    load.wait()
+    chunk = 256
+
+    @pl.loop(0, pt.shape[1] // chunk)
+    def _(i):
+        high, low = split(trail[at(i, chunk), :])
+        trail_hi[at(i, chunk), :] = high
+        trail_lo[at(i, chunk), :] = low
+
     slab_own.wait()
     for d in range(1, 8):
-        slab_recv(d).wait_recv()
+        slab_copy(d, cols[8 - d]).wait_recv()
     gram_part[...] = lax.dot_general(
         slab[...], slab[...], (((1,), (1,)), ((), ())), precision=HIGHEST, preferred_element_type=F32
     )
-
-    def gram_p_copy(d):
+    mine = y * 8 + col
+
+    def gram_p_copy(dy, dc):
+        d = dy * 8 + dc
         return remote(
-            gram_part.at[at(rem(mine + d, 32), 8)], gram_p.at[d], gp_s.at[d], gp_r.at[d], at_plane(d)
-        )
-
-    @pl.loop(1, 32)
-    def _(d):
-        gram_p_copy(d).start()
+            gram_part.at[at(ys[dy] * 8 + cols[dc], 8)], gram_p.at[d], gp_s.at[d], gp_r.at[d], at_plane(dy, dc)
+        )
+
+    for dy, dc in plane:
+        gram_p_copy(dy, dc).start()
 
     sends[0].wait_recv()
     sends[4] = remote(slot(3, 0), slot(3, 0), px_s.at[4], px_r.at[4], right)
@@ -160,110 +164,117 @@
     sends[5] = remote(slot(1, 1), slot(1, 1), px_s.at[5], px_r.at[5], left)
     sends[5].start()
     relay(1, 1, 1)
+
+    def cross_g_copy(dy, dz):
+        d = dy * 4 + dz
+        return remote(
+            cross_part.at[at(ys[dy] * 4 + near[dz], 16)], cross_g.at[d], cg_s.at[d], cg_r.at[d], at_block(dy, dz)
+        )
+
+    def cross_stage(far):
+        rows = at(chips[far], 64)
+        high, low = split(whole[rows, :])
+        dot = functools.partial(jnp.dot, preferred_element_type=F32)
+        cross_part[rows, :] = dot(high, trail_hi[...]) + (
+            dot(high, trail_lo[...]) + dot(low, trail_hi[...])
+        )
+        for dy in range(4):
+
+            @pl.when(ys[dy] == chips[far])
+            def _():
+                for dz in (2, 1, 3, 0):
+                    if dy or dz:
+                        cross_g_copy(dy, dz).start()
+
+    panel_own.wait()
+    to_twin[6].wait_recv()
+    to_twin[7].wait_recv()
+    cross_stage(0)
     sends[2].wait_recv()
     relay(2, 3, 1)
     sends[3].wait_recv()
     relay(3, 1, 0)
 
-    @pl.loop(1, 32)
-    def _(d):
-        gram_p_copy(d).wait_recv()
-
+    for dy, dc in plane:
+        gram_p_copy(dy, dc).wait_recv()
     gram_z[z] = total_of([gram_part[at(mine, 8), :]] + [gram_p[d] for d in range(1, 32)])
 
     def gram_z_copy(d, who):
         return remote(gram_z.at[z], gram_z.at[who], gz_s.at[d], gz_r.at[d], at_z(d))
 
-    for d in far_first:
+    for d in line:
         gram_z_copy(d, z).start()
 
     sends[4].wait_recv()
     relay(4, 2, 0)
     sends[5].wait_recv()
     relay(5, 2, 1)
-    panel_own.wait()
-    load.wait()
-    for i in range(8):
+    for i in range(4):
         to_twin[i].wait_recv()
-
+    cross_stage(1)
+    cross_stage(3)
+    to_twin[4].wait_recv()
+    to_twin[5].wait_recv()
+    cross_stage(2)
     keep = pltpu.make_async_copy(whole, whole_out, loc_sem.at[2])
     keep.start()
-    chunk = 512
-    cross_part[...] = jnp.zeros_like(cross_part)
-
-    @pl.loop(0, pt.shape[1] // chunk)
-    def _(i):
-        cross_part[...] += dot3(whole[:, at(i, chunk)], trail[at(i, chunk), :], ((1,), (0,)))
-
-    def cross_g_copy(d):
-        return remote(
-            cross_part.at[at(rem(group + d, 16), 16)], cross_g.at[d], cg_s.at[d], cg_r.at[d], at_group(d)
-        )
-
-    @pl.loop(1, 16)
-    def _(d):
-        cross_g_copy(d).start()
-
-    for d in range(1, 16):
-        gram_z_copy(d, rem(z + 16 - d, 16)).wait_recv()
-    gram_full[at(mine, 8), :] = total_of([gram_z[i] for i in range(16)])
-
-    def gram_f_copy(d, who):
-        return remote(
-            gram_full.at[at(mine, 8)], gram_full.at[at(who, 8)], gf_s.at[d], gf_r.at[d], at_plane(d)
-        )
-
-    @pl.loop(1, 32)
-    def _(d):
-        gram_f_copy(d, mine).start()
-
-    @pl.loop(1, 16)
-    def _(d):
-        cross_g_copy(d).wait_recv()
-
+
+    group = y * 4 + zl
+    for dy, dz in block:
+        cross_g_copy(dy, dz).wait_recv()
     cross_z[zh] = total_of([cross_part[at(group, 16), :]] + [cross_g[d] for d in range(1, 16)])
 
     def cross_z_copy(d, who):
-        where = (rem(z + 4 * d, 16) * 4 + y, col)
-        return remote(cross_z.at[zh], cross_z.at[who], cz_s.at[d], cz_r.at[d], where)
+        return remote(cross_z.at[zh], cross_z.at[who], cz_s.at[d], cz_r.at[d], at_z(4 * d))
 
     for d in (2, 1, 3):
         cross_z_copy(d, zh).start()
 
-    @pl.loop(1, 32)
-    def _(d):
-        gram_f_copy(d, rem(mine + 32 - d, 32)).wait_recv()
-
-    @pl.loop(1, 32)
-    def _(d):
-        gram_f_copy(d, mine).wait_send()
+    for d in range(1, 16):
+        gram_z_copy(d, zs[16 - d]).wait_recv()
+    gram_full[at(mine, 8), :] = total_of([gram_z[i] for i in range(16)])
+
+    def gram_f_copy(dy, dc, who):
+        d = dy * 8 + dc
+        return remote(
+            gram_full.at[at(mine, 8)], gram_full.at[at(who, 8)], gf_s.at[d], gf_r.at[d], at_plane(dy, dc)
+        )
+
+    for dy, dc in plane:
+        gram_f_copy(dy, dc, mine).start()
+
+    for dy, dc in plane:
+        gram_f_copy(dy, dc, ys[-dy] * 8 + cols[-dc]).wait_recv()
+
+    for dy, dc in plane:
+        gram_f_copy(dy, dc, mine).wait_send()
 
     order = gram_full.shape[0]
     across = lax.broadcasted_iota(jnp.int32, (order, order), 1)
     down = lax.broadcasted_iota(jnp.int32, (order, order), 0)
     lower[...] = jnp.where(down == across, 1.0, 0.0)
-    for index in range(order // STEP // 2):
+    early = 2
+    for index in range(early):
         factor_block(gram_full, lower, index)
 
     for d in range(1, 4):
         cross_z_copy(d, rem(zh + 4 - d, 4)).wait_recv()
     cross_full[at(group, 16), :] = total_of([cross_z[i] for i in range(4)])
 
-    def cross_f_copy(d, who):
+    def cross_f_copy(dy, dz, who):
+        d = dy * 4 + dz
         return remote(
-            cross_full.at[at(group, 16)], cross_full.at[at(who, 16)], cf_s.at[d], cf_r.at[d], at_group(d)
-        )
-
-    @pl.loop(1, 16)
-    def _(d):
-        cross_f_copy(d, group).start()
-
-    for index in range(order // STEP // 2, order // STEP):
+            cross_full.at[at(group, 16)], cross_full.at[at(who, 16)], cf_s.at[d], cf_r.at[d], at_block(dy, dz)
+        )
+
+    for dy, dz in block:
+        cross_f_copy(dy, dz, group).start()
+
+    for index in range(early, order // STEP):
         factor_block(gram_full, lower, index)
 
-    @pl.loop(1, 16)
-    def _(d):
-        cross_f_copy(d, rem(group + 16 - d, 16)).wait_recv()
+    for dy, dz in block:
+        cross_f_copy(dy, dz, ys[-dy] * 4 + near[-dz]).wait_recv()
 
     upper_out[...] = gram_full[...]
     lower_out[...] = lower[...]
@@ -276,19 +287,15 @@
         to_twin[i].wait_send()
     for d in range(1, 4):
         cross_z_copy(d, zh).wait_send()
-
-    @pl.loop(1, 16)
-    def _(d):
+    for d in range(1, 16):
         gram_z_copy(d, z).wait_send()
-        cross_g_copy(d).wait_send()
-        cross_f_copy(d, group).wait_send()
-
+    for dy, dz in block:
+        cross_g_copy(dy, dz).wait_send()
+        cross_f_copy(dy, dz, group).wait_send()
     for d in range(1, 8):
-        slab_copy(d).wait_send()
-
-    @pl.loop(1, 32)
-    def _(d):
-        gram_p_copy(d).wait_send()
+        slab_copy(d, col).wait_send()
+    for dy, dc in plane:
+        gram_p_copy(dy, dc).wait_send()
 
 
 def factor_block(work, lower, index):
@@ -335,6 +342,8 @@
         scratch_shapes=[
             pltpu.VMEM((256, rows), F32),
             pltpu.VMEM(trailing.shape, F32),
+            pltpu.VMEM(trailing.shape, BF16),
+            pltpu.VMEM(trailing.shape, BF16),
             pltpu.VMEM((256, 256), F32),
             pltpu.VMEM((256, 256), F32),
             pltpu.VMEM((32, 8, 256), F32),

time: 68.8 us -> 70.9 us (1.031)
  Pallas kernels: 68 us -> 70.1 us
    pallas_call x1, Pallas kernels: 64.2 us -> 66.3 us  [panel_call(): pl.pallas_call(panel_kernel, out_shape=(jax.ShapeDtypeStruct((256, rows),...]
where the time goes in v4:
time: 70.9 us; the launch traced here: 70.7 us
  Pallas kernels  70.1 us (99%)
    pallas_call x1, Pallas kernels, panel_call(): pl.pallas_call(panel_kernel, out_shape=(jax.ShapeDtypeStruct((256, rows),...  66.3 us
    pallas_call x1, Pallas kernels, update_call(): pl.pallas_call(update_kernel, out_shape=(jax.ShapeDtypeStruct((32, 256),...  3.78 us

profile of v4, /device:TPU:1, one launch (start us, length us, event | category | flops | bytes accessed | tf_op | source)
XLA Modules:
  0.0 70.7 jit_solution(5945787518377207537)
XLA Ops:
  0.6 0.0 copy-start
  0.6 66.3 %shard_map.49 = (f32[256,2048]{1,0:T(8,128)S(1)}, f32[256,256]{1,0:T(8,128)S(1)}, f32[256,256]{1,0:T(8,128)S(1)}, f32[256,256]{1,0:T(8,128)S(1)}) custom-call(f32[32,2048]{1,0:T(8,128)} %bitcast.2, f32[2048,256]{1,0:T(8,128)} %trail.1), custom_call_target="tpu_custom_call" | custom-call | tf_op jit(solution)/shard_map/pallas_call | solution.py:335
  66.9 0.0 copy-done
  66.9 3.8 %shard_map.50 = (f32[32,256]{1,0:T(8,128)}, f32[256,256]{1,0:T(8,128)}, f32[2048,256]{1,0:T(8,128)}) custom-call(f32[256,2048]{1,0:T(8,128)S(1)} %get-tuple-element.10.whole, f32[256,256]{1,0:T(8,128)S(1)} %get-tuple-element.11.upper, f32[256,256]{1,0:T(8,128)S(1)} %get-tuple-element.12.lower, f32[256,256]{1,0:T(8,128)S(1)} %get-tuple-element.13.cross, ...), custom_call_target="tpu_custom_call" | custom-call | tf_op jit(solution)/shard_map/pallas_call | solution.py:394
Async XLA Ops:
  0.6 66.3 %copy-start = (f32[2048,256]{1,0:T(8,128)S(1)}, f32[2048,256]{1,0:T(8,128)}, u32[]{:S(2)}) copy-start(f32[2048,256]{1,0:T(8,128)} %trail.1) | copy-start | bytes 6291460

commit v5 on v4

--- a/solution.py
+++ b/solution.py
@@ -11,7 +11,7 @@
 BF16 = jnp.bfloat16
 HIGHEST = lax.Precision.HIGHEST
 MESH = pl.DeviceIdType.MESH
-STEP = 16
+STEP = 32
 LANES = 128
 
 
@@ -47,11 +47,11 @@
 
 
 def panel_kernel(
-    pt, tr, whole_out, upper_out, lower_out, cross_out,
-    whole, trail, trail_hi, trail_lo, slab, gram_part, gram_p, gram_z, gram_full,
-    cross_part, cross_g, cross_z, cross_full, lower,
+    pt, tr, whole_out, work, cross_out,
+    whole, trail, trail_hi, trail_lo, slab, gram_part, gram_t, gram_p, gram_z, gram_full,
+    cross_part, cross_g, cross_z, cross_full,
     loc_sem, ps_s, ps_r, px_s, px_r, sb_s, sb_r, gp_s, gp_r, gz_s, gz_r, gf_s, gf_r,
-    cg_s, cg_r, cz_s, cz_r, cf_s, cf_r,
+    tw_s, tw_r, cg_s, cg_r, cz_s, cz_r, cf_s, cf_r,
 ):
     row, col = lax.axis_index("row"), lax.axis_index("col")
     rem, div = lax.rem, lax.div
@@ -64,12 +64,12 @@
     near = [zl] + [rem(zl + d, 4) for d in range(1, 4)]
     chips = [x] + [rem(x + d, 4) for d in range(1, 4)]
 
-    plane = [(dy, dc) for dy in (2, 1, 3, 0) for dc in (4, 3, 5, 2, 6, 1, 7, 0) if (dy, dc) != (0, 0)]
+    plane = [(dy, dx) for dy in (2, 1, 3, 0) for dx in (2, 1, 3, 0) if (dy, dx) != (0, 0)]
     block = [(dy, dz) for dz in (2, 1, 3, 0) for dy in (2, 1, 3, 0) if (dy, dz) != (0, 0)]
     line = (8, 7, 9, 6, 10, 5, 11, 4, 12, 3, 13, 2, 14, 1, 15)
 
-    def at_plane(dy, dc):
-        return (z * 4 + ys[dy], cols[dc])
+    def at_plane(dy, dx):
+        return (z * 4 + ys[dy], chips[dx] * 2 + core)
 
     def at_z(d):
         return (zs[d] * 4 + y, col)
@@ -83,9 +83,12 @@
     for dy, dz in block:
         if dy and dz:
             pl.semaphore_signal(barrier, inc=1, device_id=at_block(dy, dz), device_id_type=MESH)
-    for dy, dc in plane:
-        pl.semaphore_signal(barrier, inc=1, device_id=at_plane(dy, dc), device_id_type=MESH)
-    pl.semaphore_wait(barrier, 55)
+    for dy, dx in plane:
+        pl.semaphore_signal(barrier, inc=1, device_id=at_plane(dy, dx), device_id_type=MESH)
+    for dx in (2, 1, 3, 0):
+        where = (row, chips[dx] * 2 + 1 - core)
+        pl.semaphore_signal(barrier, inc=1, device_id=where, device_id_type=MESH)
+    pl.semaphore_wait(barrier, 43)
 
     def slab_copy(d, who):
         return remote(
@@ -145,16 +148,21 @@
     gram_part[...] = lax.dot_general(
         slab[...], slab[...], (((1,), (1,)), ((), ())), precision=HIGHEST, preferred_element_type=F32
     )
-    mine = y * 8 + col
-
-    def gram_p_copy(dy, dc):
-        d = dy * 8 + dc
+    gram_twin = remote(gram_part.at[at(1 - core, 128)], gram_t, tw_s.at[0], tw_r.at[0], twin)
+    gram_twin.start()
+    gram_twin.wait_recv()
+    gram_t[...] += gram_part[at(core, 128), :]
+    place = y * 4 + x
+    mine = core * 16 + place
+
+    def gram_p_copy(dy, dx):
+        d = dy * 4 + dx
         return remote(
-            gram_part.at[at(ys[dy] * 8 + cols[dc], 8)], gram_p.at[d], gp_s.at[d], gp_r.at[d], at_plane(dy, dc)
-        )
-
-    for dy, dc in plane:
-        gram_p_copy(dy, dc).start()
+            gram_t.at[at(ys[dy] * 4 + chips[dx], 8)], gram_p.at[d], gp_s.at[d], gp_r.at[d], at_plane(dy, dx)
+        )
+
+    for dy, dx in plane:
+        gram_p_copy(dy, dx).start()
 
     sends[0].wait_recv()
     sends[4] = remote(slot(3, 0), slot(3, 0), px_s.at[4], px_r.at[4], right)
@@ -195,9 +203,9 @@
     sends[3].wait_recv()
     relay(3, 1, 0)
 
-    for dy, dc in plane:
-        gram_p_copy(dy, dc).wait_recv()
-    gram_z[z] = total_of([gram_part[at(mine, 8), :]] + [gram_p[d] for d in range(1, 32)])
+    for dy, dx in plane:
+        gram_p_copy(dy, dx).wait_recv()
+    gram_z[z] = total_of([gram_t[at(place, 8), :]] + [gram_p[d] for d in range(1, 16)])
 
     def gram_z_copy(d, who):
         return remote(gram_z.at[z], gram_z.at[who], gz_s.at[d], gz_r.at[d], at_z(d))
@@ -220,6 +228,19 @@
     keep.start()
 
     group = y * 4 + zl
+    for d in range(1, 16):
+        gram_z_copy(d, zs[16 - d]).wait_recv()
+    gram_full[at(mine, 8), :] = total_of([gram_z[i] for i in range(16)])
+
+    def gram_f_copy(dy, dx, who):
+        d = dy * 4 + dx
+        return remote(
+            gram_full.at[at(mine, 8)], gram_full.at[at(who, 8)], gf_s.at[d], gf_r.at[d], at_plane(dy, dx)
+        )
+
+    for dy, dx in plane:
+        gram_f_copy(dy, dx, mine).start()
+
     for dy, dz in block:
         cross_g_copy(dy, dz).wait_recv()
     cross_z[zh] = total_of([cross_part[at(group, 16), :]] + [cross_g[d] for d in range(1, 16)])
@@ -230,36 +251,15 @@
     for d in (2, 1, 3):
         cross_z_copy(d, zh).start()
 
-    for d in range(1, 16):
-        gram_z_copy(d, zs[16 - d]).wait_recv()
-    gram_full[at(mine, 8), :] = total_of([gram_z[i] for i in range(16)])
-
-    def gram_f_copy(dy, dc, who):
-        d = dy * 8 + dc
-        return remote(
-            gram_full.at[at(mine, 8)], gram_full.at[at(who, 8)], gf_s.at[d], gf_r.at[d], at_plane(dy, dc)
-        )
-
-    for dy, dc in plane:
-        gram_f_copy(dy, dc, mine).start()
-
-    for dy, dc in plane:
-        gram_f_copy(dy, dc, ys[-dy] * 8 + cols[-dc]).wait_recv()
-
-    for dy, dc in plane:
-        gram_f_copy(dy, dc, mine).wait_send()
-
-    order = gram_full.shape[0]
-    across = lax.broadcasted_iota(jnp.int32, (order, order), 1)
-    down = lax.broadcasted_iota(jnp.int32, (order, order), 0)
-    lower[...] = jnp.where(down == across, 1.0, 0.0)
-    early = 2
-    for index in range(early):
-        factor_block(gram_full, lower, index)
-
-    for d in range(1, 4):
-        cross_z_copy(d, rem(zh + 4 - d, 4)).wait_recv()
-    cross_full[at(group, 16), :] = total_of([cross_z[i] for i in range(4)])
+    for dy, dx in plane:
+        gram_f_copy(dy, dx, core * 16 + ys[-dy] * 4 + chips[-dx]).wait_recv()
+
+    def full_twin(who):
+        rows = gram_full.at[at(who, 128)]
+        return remote(gram_full.at[at(core, 128)], rows, tw_s.at[1], tw_r.at[1], twin)
+
+    full_twin(core).start()
+    full_twin(1 - core).wait_recv()
 
     def cross_f_copy(dy, dz, who):
         d = dy * 4 + dz
@@ -267,17 +267,17 @@
             cross_full.at[at(group, 16)], cross_full.at[at(who, 16)], cf_s.at[d], cf_r.at[d], at_block(dy, dz)
         )
 
-    for dy, dz in block:
-        cross_f_copy(dy, dz, group).start()
-
-    for index in range(early, order // STEP):
-        factor_block(gram_full, lower, index)
+    def share_cross():
+        for d in range(1, 4):
+            cross_z_copy(d, rem(zh + 4 - d, 4)).wait_recv()
+        cross_full[at(group, 16), :] = total_of([cross_z[i] for i in range(4)])
+        for dy, dz in block:
+            cross_f_copy(dy, dz, group).start()
+
+    factor(gram_full, work, share_cross)
 
     for dy, dz in block:
         cross_f_copy(dy, dz, ys[-dy] * 4 + near[-dz]).wait_recv()
-
-    upper_out[...] = gram_full[...]
-    lower_out[...] = lower[...]
     cross_out[...] = cross_full[...]
 
     keep.wait()
@@ -294,36 +294,72 @@
         cross_f_copy(dy, dz, group).wait_send()
     for d in range(1, 8):
         slab_copy(d, col).wait_send()
-    for dy, dc in plane:
-        gram_p_copy(dy, dc).wait_send()
-
-
-def factor_block(work, lower, index):
-    order = work.shape[0]
-    start = index * STEP
-    upper_half = start < LANES
-    places = [(work, 0), (work, 1), (lower, 0)] if upper_half else [(work, 1), (lower, 0), (lower, 1)]
-    rows = jnp.concatenate([ref[start : start + STEP, LANES * q : LANES * (q + 1)] for ref, q in places], 1)
-    lane = start % LANES
+    for dy, dx in plane:
+        gram_p_copy(dy, dx).wait_send()
+        gram_f_copy(dy, dx, mine).wait_send()
+    gram_twin.wait_send()
+    full_twin(core).wait_send()
+
+
+def eliminate(rows, lane):
     down = lax.broadcasted_iota(jnp.int32, (STEP, LANES), 0)
     wide = lax.broadcasted_iota(jnp.int32, rows.shape, 0)
     columns = [jnp.broadcast_to(rows[:, lane + j : lane + j + 1], (STEP, LANES)) for j in range(STEP)]
-    for j in range(STEP):
-        scale = lax.rsqrt(columns[j][j : j + 1, :])
-        below = jnp.where(down > j, columns[j] * scale, 0.0)
-        for m in range(j + 1, STEP):
-            columns[m] = columns[m] - below * below[m : m + 1, :]
-        pivot_row = rows[j : j + 1, :] * jnp.concatenate([scale] * 3, 1)
-        rows = jnp.where(wide == j, pivot_row, rows - jnp.concatenate([below] * 3, 1) * pivot_row)
-    for i, (ref, q) in enumerate(places):
-        ref[start : start + STEP, LANES * q : LANES * (q + 1)] = rows[:, LANES * i : LANES * (i + 1)]
-    if start + STEP < order:
-        left = rows[:, start + STEP : 2 * LANES] if upper_half else rows[:, start + STEP - LANES : LANES]
-        update = lax.dot_general(
-            left, rows, (((0,), (0,)), ((), ())), precision=HIGHEST, preferred_element_type=F32
-        )
-        for i, (ref, q) in enumerate(places):
-            ref[start + STEP :, LANES * q : LANES * (q + 1)] -= update[:, LANES * i : LANES * (i + 1)]
+
+    def across(value):
+        return jnp.concatenate([value] * 3, 1)
+
+    for j in range(0, STEP, 2):
+        first, second = columns[j][j : j + 1, :], columns[j][j + 1 : j + 2, :]
+        third = columns[j + 1][j + 1 : j + 2, :]
+        scale_0 = lax.rsqrt(first)
+        scale_1 = lax.rsqrt(first * third - second * second) * (first * scale_0)
+        link = second * scale_0
+        below_0 = jnp.where(down > j, columns[j] * scale_0, 0.0)
+        below_1 = jnp.where(down > j + 1, (columns[j + 1] - below_0 * link) * scale_1, 0.0)
+        for m in range(j + 2, STEP):
+            columns[m] = columns[m] - (below_0 * below_0[m : m + 1, :] + below_1 * below_1[m : m + 1, :])
+        row_0 = rows[j : j + 1, :] * across(scale_0)
+        row_1 = (rows[j + 1 : j + 2, :] - across(link) * row_0) * across(scale_1)
+        rest = rows - (across(below_0) * row_0 + across(below_1) * row_1)
+        rows = jnp.where(wide == j, row_0, jnp.where(wide == j + 1, row_1, rest))
+    return rows
+
+
+def factor(gram, work, midway):
+    order = gram.shape[0]
+    work[...] = jnp.zeros_like(work)
+
+    def span(start):
+        return (0, 3 * LANES) if start < LANES else (LANES, 4 * LANES)
+
+    def base(start):
+        across = lax.broadcasted_iota(jnp.int32, (STEP, order), 1)
+        down = lax.broadcasted_iota(jnp.int32, (STEP, order), 0)
+        unit = jnp.where(across == down + start, 1.0, 0.0)
+        low, high = span(start)
+        return jnp.concatenate([gram[start : start + STEP, :], unit], 1)[:, low:high]
+
+    def terms(start, first, last):
+        low, high = span(start)
+        return lax.dot_general(
+            work[first:last, start : start + STEP], work[first:last, low:high],
+            (((0,), (0,)), ((), ())), precision=HIGHEST, preferred_element_type=F32,
+        )
+
+    ready = base(0)
+    for start in range(0, order, STEP):
+        later = start + STEP
+        if later < order:
+            ahead = base(later)
+            if start:
+                ahead = ahead - terms(later, 0, start)
+        low, high = span(start)
+        work[start:later, low:high] = eliminate(ready, start % LANES)
+        if start == 0:
+            midway()
+        if later < order:
+            ready = ahead - terms(later, start, later)
 
 
 def panel_call(pt, trailing):
@@ -335,10 +371,10 @@
     return pl.pallas_call(
         panel_kernel,
         out_shape=(
-            jax.ShapeDtypeStruct((256, rows), F32), square, square, square,
+            jax.ShapeDtypeStruct((256, rows), F32), jax.ShapeDtypeStruct((256, 512), F32), square,
         ),
         in_specs=[hbm, hbm],
-        out_specs=(pl.BlockSpec(memory_space=pl.ANY), vmem, vmem, vmem),
+        out_specs=(pl.BlockSpec(memory_space=pl.ANY), vmem, vmem),
         scratch_shapes=[
             pltpu.VMEM((256, rows), F32),
             pltpu.VMEM(trailing.shape, F32),
@@ -346,17 +382,17 @@
             pltpu.VMEM(trailing.shape, BF16),
             pltpu.VMEM((256, 256), F32),
             pltpu.VMEM((256, 256), F32),
-            pltpu.VMEM((32, 8, 256), F32),
+            pltpu.VMEM((128, 256), F32),
+            pltpu.VMEM((16, 8, 256), F32),
             pltpu.VMEM((16, 8, 256), F32),
             pltpu.VMEM((256, 256), F32),
             pltpu.VMEM((256, 256), F32),
             pltpu.VMEM((16, 16, 256), F32),
             pltpu.VMEM((4, 16, 256), F32),
             pltpu.VMEM((256, 256), F32),
-            pltpu.VMEM((256, 256), F32),
             dma((4,)), dma((8,)), dma((8,)),
             dma((6,)), dma((6,)), dma((8,)), dma((8,)),
-            dma((32,)), dma((32,)), dma((16,)), dma((16,)), dma((32,)), dma((32,)),
+            dma((16,)), dma((16,)), dma((16,)), dma((16,)), dma((16,)), dma((16,)), dma((2,)), dma((2,)),
             dma((16,)), dma((16,)), dma((4,)), dma((4,)), dma((16,)), dma((16,)),
         ],
         compiler_params=pltpu.CompilerParams(
@@ -365,14 +401,15 @@
     )(pltpu.with_memory_space_constraint(pt, pltpu.HBM), pltpu.with_memory_space_constraint(trailing, pltpu.HBM))
 
 
-def update_kernel(whole, upper, lower, cross, trail, factor_out, coupling_out, updated_out, scratch, block, sems):
-    order = upper.shape[0]
+def update_kernel(whole, work, cross, trail, factor_out, coupling_out, updated_out, scratch, block, sems):
+    order = work.shape[0]
+    upper, lower = work[:, :order], work[:, order:]
     across = lax.broadcasted_iota(jnp.int32, (order, order), 1)
     down = lax.broadcasted_iota(jnp.int32, (order, order), 0)
-    coupling = jnp.dot(lower[...], cross[...], precision=HIGHEST, preferred_element_type=F32)
+    coupling = jnp.dot(lower, cross[...], precision=HIGHEST, preferred_element_type=F32)
     coupling_out[...] = coupling
     solved = lax.dot_general(
-        lower[...], coupling, (((0,), (0,)), ((), ())), precision=HIGHEST, preferred_element_type=F32
+        lower, coupling, (((0,), (0,)), ((), ())), precision=HIGHEST, preferred_element_type=F32
     )
     steps, size = block.shape[0], block.shape[1]
     copies = []
@@ -381,13 +418,13 @@
         block[i] = trail[rows, :] - dot3(whole[:, rows], solved, ((0,), (0,)))
         copies.append(pltpu.make_async_copy(block.at[i], updated_out.at[pl.ds(i * size, size)], sems.at[i]))
         copies[-1].start()
-    scratch[...] = jnp.where(across >= down, upper[...], 0.0).T
+    scratch[...] = jnp.where(across >= down, upper, 0.0).T
     factor_out[...] = scratch[at(lax.axis_index("col"), 32), :]
     for copy in copies:
         copy.wait()
 
 
-def update_call(whole_t, upper, lower, cross, trailing):
+def update_call(whole_t, work, cross, trailing):
     rows, width = trailing.shape
     vmem = pl.BlockSpec(memory_space=pltpu.VMEM)
     steps = 8
@@ -397,7 +434,7 @@
             jax.ShapeDtypeStruct((32, 256), F32), jax.ShapeDtypeStruct((256, width), F32),
             jax.ShapeDtypeStruct((rows, width), F32),
         ),
-        in_specs=[vmem] * 5,
+        in_specs=[vmem] * 4,
         out_specs=(vmem, vmem, pl.BlockSpec(memory_space=pl.ANY)),
         scratch_shapes=[
             pltpu.VMEM((256, 256), F32),
@@ -405,12 +442,12 @@
             pltpu.SemaphoreType.DMA((steps,)),
         ],
         compiler_params=pltpu.CompilerParams(vmem_limit_bytes=40 * 2**20),
-    )(whole_t, upper, lower, cross, trailing)
+    )(whole_t, work, cross, trailing)
 
 
 def on_device(panel, trailing):
-    whole_t, upper, lower, cross = panel_call(panel.T, trailing)
-    factor_t, coupling, updated = update_call(whole_t, upper, lower, cross, trailing)
+    whole_t, work, cross = panel_call(panel.T, trailing)
+    factor_t, coupling, updated = update_call(whole_t, work, cross, trailing)
     return factor_t.T, coupling, updated
 
 

time: 70.9 us -> 62.5 us (0.88)
  the two profiles are of different devices: /device:TPU:1 before, /device:TPU:32 now
where the time goes in v5:
time: 62.5 us; the launch traced here: 62.3 us
  Pallas kernels  61.7 us (99%)
  between operations  0.65 us (1%)
    pallas_call x1, Pallas kernels, panel_call(): pl.pallas_call(panel_kernel, out_shape=(jax.ShapeDtypeStruct((256, rows),...  57.9 us
    pallas_call x1, Pallas kernels, update_call(): pl.pallas_call(update_kernel, out_shape=(jax.ShapeDtypeStruct((32, 256),...  3.76 us

profile of v5, /device:TPU:32, one launch (start us, length us, event | category | flops | bytes accessed | tf_op | source)
XLA Modules:
  0.0 62.3 jit_solution(17715438746134671019)
XLA Ops:
  0.6 0.0 copy-start
  0.6 57.9 %shard_map.49 = (f32[256,2048]{1,0:T(8,128)S(1)}, f32[256,512]{1,0:T(8,128)S(1)}, f32[256,256]{1,0:T(8,128)S(1)}) custom-call(f32[32,2048]{1,0:T(8,128)} %bitcast.2, f32[2048,256]{1,0:T(8,128)} %trail.1), custom_call_target="tpu_custom_call" | custom-call | tf_op jit(solution)/shard_map/pallas_call | solution.py:371
  58.6 0.0 copy-done
  58.6 3.8 %shard_map.50 = (f32[32,256]{1,0:T(8,128)}, f32[256,256]{1,0:T(8,128)}, f32[2048,256]{1,0:T(8,128)}) custom-call(f32[256,2048]{1,0:T(8,128)S(1)} %get-tuple-element.9.whole, f32[256,512]{1,0:T(8,128)S(1)} %get-tuple-element.10.work, f32[256,256]{1,0:T(8,128)S(1)} %get-tuple-element.11.cross, f32[2048,256]{1,0:T(8,128)S(1)} %copy-done), custom_call_target="tpu_custom_call" | custom-call | tf_op jit(solution)/shard_map/pallas_call | solution.py:431
Async XLA Ops:
  0.6 57.9 %copy-start = (f32[2048,256]{1,0:T(8,128)S(1)}, f32[2048,256]{1,0:T(8,128)}, u32[]{:S(2)}) copy-start(f32[2048,256]{1,0:T(8,128)} %trail.1) | copy-start | bytes 6291460

commit v6 on v5

--- a/solution.py
+++ b/solution.py
@@ -21,15 +21,6 @@
     return high, low
 
 
-def dot3(left, right, dims):
-    left_hi, left_lo = split(left)
-    right_hi, right_lo = split(right)
-    dot = functools.partial(
-        lax.dot_general, dimension_numbers=(dims, ((), ())), preferred_element_type=F32
-    )
-    return dot(left_hi, right_hi) + (dot(left_hi, right_lo) + dot(left_lo, right_hi))
-
-
 def remote(src, dst, send, recv, where):
     return pltpu.make_async_remote_copy(
         src_ref=src, dst_ref=dst, send_sem=send, recv_sem=recv, device_id=where, device_id_type=MESH
@@ -47,11 +38,11 @@
 
 
 def panel_kernel(
-    pt, tr, whole_out, work, cross_out,
+    pt, tr, high_out, low_out, work, cross_out,
     whole, trail, trail_hi, trail_lo, slab, gram_part, gram_t, gram_p, gram_z, gram_full,
     cross_part, cross_g, cross_z, cross_full,
     loc_sem, ps_s, ps_r, px_s, px_r, sb_s, sb_r, gp_s, gp_r, gz_s, gz_r, gf_s, gf_r,
-    tw_s, tw_r, cg_s, cg_r, cz_s, cz_r, cf_s, cf_r,
+    tw_s, tw_r, cg_s, cg_r, cz_s, cz_r, cf_s, cf_r, known,
 ):
     row, col = lax.axis_index("row"), lax.axis_index("col")
     rem, div = lax.rem, lax.div
@@ -78,17 +69,18 @@
         return (zh * 16 + near[dz] * 4 + ys[dy], col)
 
     barrier = pltpu.get_barrier_semaphore()
-    for d in line:
-        pl.semaphore_signal(barrier, inc=1, device_id=at_z(d), device_id_type=MESH)
-    for dy, dz in block:
-        if dy and dz:
-            pl.semaphore_signal(barrier, inc=1, device_id=at_block(dy, dz), device_id_type=MESH)
-    for dy, dx in plane:
-        pl.semaphore_signal(barrier, inc=1, device_id=at_plane(dy, dx), device_id_type=MESH)
     for dx in (2, 1, 3, 0):
         where = (row, chips[dx] * 2 + 1 - core)
         pl.semaphore_signal(barrier, inc=1, device_id=where, device_id_type=MESH)
-    pl.semaphore_wait(barrier, 43)
+    for dy, dx in plane[::-1]:
+        pl.semaphore_signal(barrier, inc=1, device_id=at_plane(dy, dx), device_id_type=MESH)
+    for d in (1, 15):
+        pl.semaphore_signal(barrier, inc=1, device_id=at_z(d), device_id_type=MESH)
+    pl.semaphore_wait(barrier, 21)
+
+    def pass_on(i):
+        for d in (2**i, 16 - 2**i):
+            pl.semaphore_signal(known.at[i], inc=1, device_id=at_z(d), device_id_type=MESH)
 
     def slab_copy(d, who):
         return remote(
@@ -133,6 +125,7 @@
     load = pltpu.make_async_copy(tr, trail, loc_sem.at[1])
     load.start()
 
+    pass_on(0)
     load.wait()
     chunk = 256
 
@@ -142,6 +135,8 @@
         trail_hi[at(i, chunk), :] = high
         trail_lo[at(i, chunk), :] = low
 
+    pl.semaphore_wait(known.at[0], 2)
+    pass_on(1)
     slab_own.wait()
     for d in range(1, 8):
         slab_copy(d, cols[8 - d]).wait_recv()
@@ -164,6 +159,8 @@
     for dy, dx in plane:
         gram_p_copy(dy, dx).start()
 
+    pl.semaphore_wait(known.at[1], 2)
+    pass_on(2)
     sends[0].wait_recv()
     sends[4] = remote(slot(3, 0), slot(3, 0), px_s.at[4], px_r.at[4], right)
     sends[4].start()
@@ -210,6 +207,7 @@
     def gram_z_copy(d, who):
         return remote(gram_z.at[z], gram_z.at[who], gz_s.at[d], gz_r.at[d], at_z(d))
 
+    pl.semaphore_wait(known.at[2], 2)
     for d in line:
         gram_z_copy(d, z).start()
 
@@ -224,8 +222,6 @@
     to_twin[4].wait_recv()
     to_twin[5].wait_recv()
     cross_stage(2)
-    keep = pltpu.make_async_copy(whole, whole_out, loc_sem.at[2])
-    keep.start()
 
     group = y * 4 + zl
     for d in range(1, 16):
@@ -250,6 +246,12 @@
 
     for d in (2, 1, 3):
         cross_z_copy(d, zh).start()
+
+    @pl.loop(0, pt.shape[1] // chunk)
+    def _(i):
+        high, low = split(whole[:, at(i, chunk)].T)
+        high_out[at(i, chunk), :] = high
+        low_out[at(i, chunk), :] = low
 
     for dy, dx in plane:
         gram_f_copy(dy, dx, core * 16 + ys[-dy] * 4 + chips[-dx]).wait_recv()
@@ -280,7 +282,6 @@
         cross_f_copy(dy, dz, ys[-dy] * 4 + near[-dz]).wait_recv()
     cross_out[...] = cross_full[...]
 
-    keep.wait()
     for i in range(6):
         sends[i].wait_send()
     for i in range(8):
@@ -371,10 +372,11 @@
     return pl.pallas_call(
         panel_kernel,
         out_shape=(
-            jax.ShapeDtypeStruct((256, rows), F32), jax.ShapeDtypeStruct((256, 512), F32), square,
+            jax.ShapeDtypeStruct((rows, 256), BF16), jax.ShapeDtypeStruct((rows, 256), BF16),
+            jax.ShapeDtypeStruct((256, 512), F32), square,
         ),
         in_specs=[hbm, hbm],
-        out_specs=(pl.BlockSpec(memory_space=pl.ANY), vmem, vmem),
+        out_specs=(vmem, vmem, vmem, vmem),
         scratch_shapes=[
             pltpu.VMEM((256, rows), F32),
             pltpu.VMEM(trailing.shape, F32),
@@ -394,6 +396,7 @@
             dma((6,)), dma((6,)), dma((8,)), dma((8,)),
             dma((16,)), dma((16,)), dma((16,)), dma((16,)), dma((16,)), dma((16,)), dma((2,)), dma((2,)),
             dma((16,)), dma((16,)), dma((4,)), dma((4,)), dma((16,)), dma((16,)),
+            pltpu.SemaphoreType.REGULAR((3,)),
         ],
         compiler_params=pltpu.CompilerParams(
             collective_id=0, has_side_effects=True, vmem_limit_bytes=40 * 2**20
@@ -401,7 +404,7 @@
     )(pltpu.with_memory_space_constraint(pt, pltpu.HBM), pltpu.with_memory_space_constraint(trailing, pltpu.HBM))
 
 
-def update_kernel(whole, work, cross, trail, factor_out, coupling_out, updated_out, scratch, block, sems):
+def update_kernel(whole_hi, whole_lo, work, cross, trail, factor_out, coupling_out, updated_out, scratch, block, sems):
     order = work.shape[0]
     upper, lower = work[:, :order], work[:, order:]
     across = lax.broadcasted_iota(jnp.int32, (order, order), 1)
@@ -411,11 +414,14 @@
     solved = lax.dot_general(
         lower, coupling, (((0,), (0,)), ((), ())), precision=HIGHEST, preferred_element_type=F32
     )
+    solved_hi, solved_lo = split(solved)
+    dot = functools.partial(jnp.dot, preferred_element_type=F32)
     steps, size = block.shape[0], block.shape[1]
     copies = []
     for i in range(steps):
         rows = slice(i * size, (i + 1) * size)
-        block[i] = trail[rows, :] - dot3(whole[:, rows], solved, ((0,), (0,)))
+        high, low = whole_hi[rows, :], whole_lo[rows, :]
+        block[i] = trail[rows, :] - (dot(high, solved_hi) + (dot(high, solved_lo) + dot(low, solved_hi)))
         copies.append(pltpu.make_async_copy(block.at[i], updated_out.at[pl.ds(i * size, size)], sems.at[i]))
         copies[-1].start()
     scratch[...] = jnp.where(across >= down, upper, 0.0).T
@@ -424,7 +430,7 @@
         copy.wait()
 
 
-def update_call(whole_t, work, cross, trailing):
+def update_call(whole_hi, whole_lo, work, cross, trailing):
     rows, width = trailing.shape
     vmem = pl.BlockSpec(memory_space=pltpu.VMEM)
     steps = 8
@@ -434,7 +440,7 @@
             jax.ShapeDtypeStruct((32, 256), F32), jax.ShapeDtypeStruct((256, width), F32),
             jax.ShapeDtypeStruct((rows, width), F32),
         ),
-        in_specs=[vmem] * 4,
+        in_specs=[vmem] * 5,
         out_specs=(vmem, vmem, pl.BlockSpec(memory_space=pl.ANY)),
         scratch_shapes=[
             pltpu.VMEM((256, 256), F32),
@@ -442,12 +448,12 @@
             pltpu.SemaphoreType.DMA((steps,)),
         ],
         compiler_params=pltpu.CompilerParams(vmem_limit_bytes=40 * 2**20),
-    )(whole_t, work, cross, trailing)
+    )(whole_hi, whole_lo, work, cross, trailing)
 
 
 def on_device(panel, trailing):
-    whole_t, work, cross = panel_call(panel.T, trailing)
-    factor_t, coupling, updated = update_call(whole_t, work, cross, trailing)
+    parts = panel_call(panel.T, trailing)
+    factor_t, coupling, updated = update_call(*parts, trailing)
     return factor_t.T, coupling, updated
 
 

time: 62.5 us -> 61.7 us (0.987)
  the two profiles are of different devices: /device:TPU:32 before, /device:TPU:14 now
where the time goes in v6:
time: 61.7 us; the launch traced here: 61.5 us
  Pallas kernels  60.9 us (99%)
  between operations  0.65 us (1%)
    pallas_call x1, Pallas kernels, panel_call(): pl.pallas_call(panel_kernel, out_shape=(jax.ShapeDtypeStruct((rows, 256),...  57.2 us
    pallas_call x1, Pallas kernels, update_call(): pl.pallas_call(update_kernel, out_shape=(jax.ShapeDtypeStruct((32, 256),...  3.72 us

profile of v6, /device:TPU:14, one launch (start us, length us, event | category | flops | bytes accessed | tf_op | source)
XLA Modules:
  0.0 61.5 jit_solution(15535974766385532681)
XLA Ops:
  0.6 0.0 copy-start
  0.6 57.2 %shard_map.49 = (bf16[2048,256]{1,0:T(8,128)(2,1)S(1)}, bf16[2048,256]{1,0:T(8,128)(2,1)S(1)}, f32[256,512]{1,0:T(8,128)S(1)}, f32[256,256]{1,0:T(8,128)S(1)}) custom-call(f32[32,2048]{1,0:T(8,128)} %bitcast.2, f32[2048,256]{1,0:T(8,128)} %trail.1), custom_call_target="tpu_custom_call" | custom-call | tf_op jit(solution)/shard_map/pallas_call | solution.py:372
  57.8 0.0 copy-done
  57.8 3.7 %shard_map.50 = (f32[32,256]{1,0:T(8,128)}, f32[256,256]{1,0:T(8,128)}, f32[2048,256]{1,0:T(8,128)}) custom-call(bf16[2048,256]{1,0:T(8,128)(2,1)S(1)} %get-tuple-element.10.whole_hi, bf16[2048,256]{1,0:T(8,128)(2,1)S(1)} %get-tuple-element.11.whole_lo, f32[256,512]{1,0:T(8,128)S(1)} %get-tuple-element.12.work, f32[256,256]{1,0:T(8,128)S(1)} %get-tuple-element.13.cross, ...), custom_call_target="tpu_custom_call" | custom-call | tf_op jit(solution)/shard_map/pallas_call | solution.py:437
Async XLA Ops:
  0.6 57.2 %copy-start = (f32[2048,256]{1,0:T(8,128)S(1)}, f32[2048,256]{1,0:T(8,128)}, u32[]{:S(2)}) copy-start(f32[2048,256]{1,0:T(8,128)} %trail.1) | copy-start | bytes 6291460

commit v7 on v6

--- a/solution.py
+++ b/solution.py
@@ -19,6 +19,15 @@
     high = value.astype(BF16)
     low = (value - high.astype(F32)).astype(BF16)
     return high, low
+
+
+def dot3(left, right, dims):
+    left_hi, left_lo = split(left)
+    right_hi, right_lo = split(right)
+    dot = functools.partial(
+        lax.dot_general, dimension_numbers=(dims, ((), ())), preferred_element_type=F32
+    )
+    return dot(left_hi, right_hi) + (dot(left_hi, right_lo) + dot(left_lo, right_hi))
 
 
 def remote(src, dst, send, recv, where):
@@ -108,8 +117,6 @@
         2: remote(own(1), slot(0, 1), px_s.at[2], px_r.at[2], right),
         3: remote(own(0), slot(0, 0), px_s.at[3], px_r.at[3], left),
     }
-    for i in range(4):
-        sends[i].start()
     to_twin = {}
 
     def relay(i, far, part, src=None):
@@ -126,6 +133,10 @@
     load.start()
 
     pass_on(0)
+    for d in range(1, 8):
+        slab_copy(d, col).wait_send()
+    for i in range(4):
+        sends[i].start()
     load.wait()
     chunk = 256
 
@@ -224,34 +235,34 @@
     cross_stage(2)
 
     group = y * 4 + zl
-    for d in range(1, 16):
-        gram_z_copy(d, zs[16 - d]).wait_recv()
-    gram_full[at(mine, 8), :] = total_of([gram_z[i] for i in range(16)])
-
-    def gram_f_copy(dy, dx, who):
-        d = dy * 4 + dx
-        return remote(
-            gram_full.at[at(mine, 8)], gram_full.at[at(who, 8)], gf_s.at[d], gf_r.at[d], at_plane(dy, dx)
-        )
-
-    for dy, dx in plane:
-        gram_f_copy(dy, dx, mine).start()
-
-    for dy, dz in block:
-        cross_g_copy(dy, dz).wait_recv()
-    cross_z[zh] = total_of([cross_part[at(group, 16), :]] + [cross_g[d] for d in range(1, 16)])
-
-    def cross_z_copy(d, who):
-        return remote(cross_z.at[zh], cross_z.at[who], cz_s.at[d], cz_r.at[d], at_z(4 * d))
-
-    for d in (2, 1, 3):
-        cross_z_copy(d, zh).start()
-
     @pl.loop(0, pt.shape[1] // chunk)
     def _(i):
         high, low = split(whole[:, at(i, chunk)].T)
         high_out[at(i, chunk), :] = high
         low_out[at(i, chunk), :] = low
+
+    for d in range(1, 16):
+        gram_z_copy(d, zs[16 - d]).wait_recv()
+    gram_full[at(mine, 8), :] = total_of([gram_z[i] for i in range(16)])
+
+    def gram_f_copy(dy, dx, who):
+        d = dy * 4 + dx
+        return remote(
+            gram_full.at[at(mine, 8)], gram_full.at[at(who, 8)], gf_s.at[d], gf_r.at[d], at_plane(dy, dx)
+        )
+
+    for dy, dx in plane:
+        gram_f_copy(dy, dx, mine).start()
+
+    for dy, dz in block:
+        cross_g_copy(dy, dz).wait_recv()
+    cross_z[zh] = total_of([cross_part[at(group, 16), :]] + [cross_g[d] for d in range(1, 16)])
+
+    def cross_z_copy(d, who):
+        return remote(cross_z.at[zh], cross_z.at[who], cz_s.at[d], cz_r.at[d], at_z(4 * d))
+
+    for d in (2, 1, 3):
+        cross_z_copy(d, zh).start()
 
     for dy, dx in plane:
         gram_f_copy(dy, dx, core * 16 + ys[-dy] * 4 + chips[-dx]).wait_recv()
@@ -293,8 +304,6 @@
     for dy, dz in block:
         cross_g_copy(dy, dz).wait_send()
         cross_f_copy(dy, dz, group).wait_send()
-    for d in range(1, 8):
-        slab_copy(d, col).wait_send()
     for dy, dx in plane:
         gram_p_copy(dy, dx).wait_send()
         gram_f_copy(dy, dx, mine).wait_send()
@@ -409,11 +418,9 @@
     upper, lower = work[:, :order], work[:, order:]
     across = lax.broadcasted_iota(jnp.int32, (order, order), 1)
     down = lax.broadcasted_iota(jnp.int32, (order, order), 0)
-    coupling = jnp.dot(lower, cross[...], precision=HIGHEST, preferred_element_type=F32)
+    coupling = dot3(lower, cross[...], ((1,), (0,)))
     coupling_out[...] = coupling
-    solved = lax.dot_general(
-        lower, coupling, (((0,), (0,)), ((), ())), precision=HIGHEST, preferred_element_type=F32
-    )
+    solved = dot3(lower, coupling, ((0,), (0,)))
     solved_hi, solved_lo = split(solved)
     dot = functools.partial(jnp.dot, preferred_element_type=F32)
     steps, size = block.shape[0], block.shape[1]

time: 61.7 us -> 60.4 us (0.979)
  the two profiles are of different devices: /device:TPU:14 before, /device:TPU:4 now
where the time goes in v7:
time: 60.4 us; the launch traced here: 60.3 us
  Pallas kernels  59.6 us (99%)
  between operations  0.65 us (1%)
    pallas_call x1, Pallas kernels, panel_call(): pl.pallas_call(panel_kernel, out_shape=(jax.ShapeDtypeStruct((rows, 256),...  56.4 us
    pallas_call x1, Pallas kernels, update_call(): pl.pallas_call(update_kernel, out_shape=(jax.ShapeDtypeStruct((32, 256),...  3.3 us

profile of v7, /device:TPU:4, one launch (start us, length us, event | category | flops | bytes accessed | tf_op | source)
XLA Modules:
  0.0 60.3 jit_solution(3161591334175808436)
XLA Ops:
  0.6 0.0 copy-start
  0.6 56.4 %shard_map.49 = (bf16[2048,256]{1,0:T(8,128)(2,1)S(1)}, bf16[2048,256]{1,0:T(8,128)(2,1)S(1)}, f32[256,512]{1,0:T(8,128)S(1)}, f32[256,256]{1,0:T(8,128)S(1)}) custom-call(f32[32,2048]{1,0:T(8,128)} %bitcast.2, f32[2048,256]{1,0:T(8,128)} %trail.1), custom_call_target="tpu_custom_call" | custom-call | tf_op jit(solution)/shard_map/pallas_call | solution.py:381
  57.0 0.0 copy-done
  57.0 3.3 %shard_map.50 = (f32[32,256]{1,0:T(8,128)}, f32[256,256]{1,0:T(8,128)}, f32[2048,256]{1,0:T(8,128)}) custom-call(bf16[2048,256]{1,0:T(8,128)(2,1)S(1)} %get-tuple-element.10.whole_hi, bf16[2048,256]{1,0:T(8,128)(2,1)S(1)} %get-tuple-element.11.whole_lo, f32[256,512]{1,0:T(8,128)S(1)} %get-tuple-element.12.work, f32[256,256]{1,0:T(8,128)S(1)} %get-tuple-element.13.cross, ...), custom_call_target="tpu_custom_call" | custom-call | tf_op jit(solution)/shard_map/pallas_call | solution.py:444
Async XLA Ops:
  0.6 56.4 %copy-start = (f32[2048,256]{1,0:T(8,128)S(1)}, f32[2048,256]{1,0:T(8,128)}, u32[]{:S(2)}) copy-start(f32[2048,256]{1,0:T(8,128)} %trail.1) | copy-start | bytes 6291460
